TPU v7x, 128 devices: a whole 4x4x4 slice. The times are simulated.
128 devices in a mesh: row: 8 (over x, z_hi), col: 16 (over y, z_lo, core).
Axes of the slice: x: 4, y: 4, z: 4 (z_hi: 2, z_lo: 2; z = z_hi * 2 + z_lo), core: 2. Of those that a mesh axis runs over, the one named last changes fastest.
Arguments:
- tokens: bfloat16 [2048, 6144], P('col', 'row'), may hold values from -7.5 to 7.5
- ln_gain: float32 [6144], P('row'), may hold values from 0.1 to 1.9
- w_qkv: bfloat16 [6144, 3, 6144], P('row', None, 'col'), may hold values from -0.078125 to 0.078125
- w_up: bfloat16 [6144, 24576], P('row', 'col'), may hold values from -0.078125 to 0.078125
- w_out: bfloat16 [6144, 6144], P('col', 'row'), may hold values from -0.078125 to 0.078125
- w_down: bfloat16 [24576, 6144], P('col', 'row'), may hold values from -0.0390625 to 0.0390625
Outputs:
- layer_out: bfloat16 [2048, 6144], P('col', 'row')
All inputs are finite; a program needn't handle non-finite values.
Results may differ from a plain program's by a relative error of at most 0.022.
Values may be sent and summed in bfloat16 or wider, within the bound.
A program may use at most 64 MiB of HBM per device.

v0:
```python
import jax
import jax.numpy as jnp
from jax import lax
from jax.sharding import PartitionSpec as P

D = 6144
HD = 128
PATCH = 256


epsilon = 1e-06


def centred(values, average, square):
    return (values - average) * lax.rsqrt(square - average * average + epsilon)


def partial_moments(values):
    widened = values.astype(jnp.float32)
    return (jnp.sum(widened, axis=-1), jnp.sum(widened * widened, axis=-1))


def apply_norm(values, linear_sum, square_sum, gain_row):
    average = linear_sum[:, None] / D
    square = square_sum[:, None] / D
    return (centred(values.astype(jnp.float32), average, square) * gain_row).astype(jnp.bfloat16)


def head_norm(values):
    average = jnp.mean(values, axis=-1, keepdims=True)
    square = jnp.mean(values * values, axis=-1, keepdims=True)
    return centred(values, average, square)


def body(tokens, ln_gain, w_qkv, w_up, w_out, w_down):
    linear_sum, square_sum = partial_moments(tokens)
    linear_sum, square_sum = lax.psum((linear_sum, square_sum), "row")
    normed = apply_norm(tokens, linear_sum, square_sum, ln_gain)
    gathered = lax.all_gather(normed, "col", axis=0, tiled=True)
    row_count = gathered.shape[0] // lax.axis_size("row")
    qkv_weight = w_qkv.reshape(w_qkv.shape[0], -1)
    qkv_width = qkv_weight.shape[1]

    def rows_of():
        return gathered

    qkv_sum = lax.psum_scatter(
        jnp.dot(rows_of(), qkv_weight, preferred_element_type=jnp.float32).astype(jnp.bfloat16),
        "row",
        scatter_dimension=0,
        tiled=True,
    ).astype(jnp.float32)
    up_sum = lax.psum_scatter(
        jnp.dot(rows_of(), w_up, preferred_element_type=jnp.float32).astype(jnp.bfloat16),
        "row",
        scatter_dimension=0,
        tiled=True,
    ).astype(jnp.float32)
    heads_here = qkv_width // (3 * HD)
    image_blocks = qkv_sum.reshape(row_count // PATCH, PATCH, 3, heads_here, HD)
    queries = head_norm(image_blocks[:, :, 0]).astype(jnp.bfloat16)
    key_norm = head_norm(image_blocks[:, :, 1]).astype(jnp.bfloat16)
    values = image_blocks[:, :, 2].astype(jnp.bfloat16)
    scores = jnp.einsum(
        "iphe,iqhe->ihpq", queries, key_norm, preferred_element_type=jnp.float32
    ) * HD ** (-0.5)
    weights = jnp.exp(scores)
    probabilities = (weights / jnp.sum(weights, axis=-1, keepdims=True)).astype(jnp.bfloat16)
    attended = jnp.einsum(
        "ihpq,iqhe->iphe", probabilities, values, preferred_element_type=jnp.float32
    )
    attended = attended.astype(jnp.bfloat16).reshape(row_count, heads_here * HD)
    hidden = jax.nn.gelu(up_sum, approximate=True).astype(jnp.bfloat16)
    attended_all, hidden_all = (
        lax.all_gather(attended, "row", axis=0, tiled=True),
        lax.all_gather(hidden, "row", axis=0, tiled=True),
    )
    branch = lax.psum_scatter(
        (
            jnp.dot(attended_all, w_out, preferred_element_type=jnp.float32)
            + jnp.dot(hidden_all, w_down, preferred_element_type=jnp.float32)
        ).astype(jnp.bfloat16),
        "col",
        scatter_dimension=0,
        tiled=True,
    ).astype(jnp.float32)
    return (tokens.astype(jnp.float32) + branch).astype(jnp.bfloat16)


def solution(mesh):
    return jax.shard_map(
        body,
        mesh=mesh,
        in_specs=(
            P("col", "row"),
            P("row"),
            P("row", None, "col"),
            P("row", "col"),
            P("col", "row"),
            P("col", "row"),
        ),
        out_specs=P("col", "row"),
        check_vma=False,
    )
```

profile of v0, /device:TPU:0, one launch (start us, length us, event | category | flops | bytes accessed | tf_op | source)
XLA Modules:
  0.0 490.1 jit_solution(16779165526972222839)
XLA Ops:
  6.5 0.0 copy-start
  6.5 0.0 all-gather.4.cloned.1.call-start
  6.5 1.2 convert_reduce_fusion
  7.7 25.1 %all-reduce = (f32[128]{0:T(128)S(1)}, f32[128]{0:T(128)S(1)}) all-reduce(f32[128]{0:T(128)S(1)} %get-tuple-element.10, f32[128]{0:T(128)S(1)} %get-tuple-element.9), channel_id=1, replica_groups=mesh['row'=8,'col'=16] {'row'}, use_global_device_ids=true, to_apply=%region_3.0 | all-reduce | flops 256 | bytes 2048 | tf_op jit(solution)/shard_map/psum | solution.py:37
  32.9 1.8 fusion.9
  34.6 0.0 all-gather.4.cloned.1.call-update
  34.7 0.0 reduce-scatter.6.cloned.1.call-start
  34.7 32.8 %all-gather.4.cloned.1.call-done = bf16[2048,768]{1,0:T(8,128)(2,1)} async-done(((bf16[128,768]{1,0:T(8,128)(2,1)}), bf16[2048,768]{1,0:T(8,128)(2,1)}) %all-gather.4.cloned.1.call-update) | async-done | bytes 3145744 | tf_op jit(solution)/shard_map/all_gather | solution.py:39
  67.5 0.0 copy-done
  67.5 8.9 %convolution_convert_fusion = bf16[2048,1536]{1,0:T(8,128)(2,1)} fusion(bf16[2048,768]{1,0:T(8,128)(2,1)} %all-gather.4.cloned.1.call-done, bf16[768,1536]{1,0:T(8,128)(2,1)S(1)} %copy-done), kind=kOutput, calls=%fused_computation | convolution fusion | flops 4834983936 | bytes 11796480 | tf_op jit(solution)/shard_map/dot_general | solution.py:54
  76.4 0.0 reduce-scatter.6.cloned.1.call-update
  76.4 0.0 reduce-scatter.4.cloned.1.call-start
  76.4 3.8 copy.10
  80.3 8.9 %convolution_convert_fusion.1 = bf16[2048,1152]{1,0:T(8,128)(2,1)} fusion(bf16[2048,768]{1,0:T(8,128)(2,1)} %all-gather.4.cloned.1.call-done, bf16[768,1152]{0,1:T(8,128)(2,1)} %bitcast.35), kind=kOutput, calls=%fused_computation.1 | convolution fusion | flops 3626237952 | bytes 9633792 | tf_op jit(solution)/shard_map/dot_general | solution.py:48
  89.2 0.0 reduce-scatter.4.cloned.1.call-update
  89.2 0.0 all-gather.8.cloned.1.call-start
  89.3 86.8 %reduce-scatter.6.cloned.1.call-done = bf16[256,1536]{1,0:T(8,128)(2,1)} async-done(((bf16[2048,1536]{1,0:T(8,128)(2,1)}), bf16[256,1536]{1,0:T(8,128)(2,1)}) %reduce-scatter.6.cloned.1.call-update) | async-done | bytes 786448 | tf_op jit(solution)/shard_map/reduce_scatter | solution.py:53
  176.1 2.6 fusion.5
  178.7 0.0 all-gather.8.cloned.1.call-update
  178.7 0.0 all-gather.6.cloned.1.call-start
  178.8 88.6 %reduce-scatter.4.cloned.1.call-done = bf16[256,1152]{1,0:T(8,128)(2,1)} async-done(((bf16[2048,1152]{1,0:T(8,128)(2,1)}), bf16[256,1152]{1,0:T(8,128)(2,1)}) %reduce-scatter.4.cloned.1.call-update) | async-done | bytes 589840 | tf_op jit(solution)/shard_map/reduce_scatter | solution.py:47
  267.4 1.3 copy.11
  268.7 0.1 reshape.141
  268.8 0.1 slice_reduce_fusion.1
  268.9 1.2 fusion.6
  270.1 2.3 convolution_convert_fusion.2
  272.5 0.0 all-gather.6.cloned.1.call-update
  272.5 0.0 copy-start.2
  272.5 0.2 reduce-scatter.8.cloned.1.call-start
  272.8 85.0 %all-gather.8.cloned.1.call-done = bf16[2048,1536]{1,0:T(8,128)(2,1)} async-done(((bf16[256,1536]{1,0:T(8,128)(2,1)}), bf16[2048,1536]{1,0:T(8,128)(2,1)}) %all-gather.8.cloned.1.call-update) | async-done | bytes 6291472 | tf_op jit(solution)/shard_map/all_gather | solution.py:76
  357.8 9.5 %fusion.24 = f32[2048,768]{1,0:T(8,128)} fusion(bf16[2048,1536]{1,0:T(8,128)(2,1)} %all-gather.8.cloned.1.call-done, bf16[1536,768]{1,0:T(8,128)(2,1)} %param.11), kind=kOutput, calls=%fused_computation.49 | convolution fusion | flops 4831838208 | bytes 14942208 | tf_op jit(solution)/shard_map/dot_general | solution.py:81
  367.2 43.1 %all-gather.6.cloned.1.call-done = bf16[2048,384]{0,1:T(8,128)(2,1)} async-done(((bf16[256,384]{0,1:T(8,128)(2,1)}), bf16[2048,384]{0,1:T(8,128)(2,1)}) %all-gather.6.cloned.1.call-update) | async-done | bytes 1572880 | tf_op jit(solution)/shard_map/all_gather | solution.py:75
  410.3 0.0 copy-done.2
  410.3 6.8 %add_convert_fusion = bf16[2048,768]{1,0:T(8,128)(2,1)} fusion(f32[2048,768]{1,0:T(8,128)} %fusion.24, bf16[2048,384]{0,1:T(8,128)(2,1)} %all-gather.6.cloned.1.call-done, bf16[384,768]{1,0:T(8,128)(2,1)S(1)} %copy-done.2), kind=kOutput, calls=%fused_computation.2 | convolution fusion | flops 1211105280 | bytes 11599872 | tf_op jit(solution)/shard_map/dot_general | solution.py:80
  417.1 0.0 copy-start.1
  417.1 0.0 reduce-scatter.8.cloned.1.call-update
  417.1 64.5 %reduce-scatter.8.cloned.1.call-done = bf16[128,768]{1,0:T(8,128)(2,1)} async-done(((bf16[2048,768]{1,0:T(8,128)(2,1)}), bf16[128,768]{1,0:T(8,128)(2,1)}) %reduce-scatter.8.cloned.1.call-update) | async-done | bytes 196624 | tf_op jit(solution)/shard_map/reduce_scatter | solution.py:78
  481.6 0.0 copy-done.1
  481.6 1.6 fusion.11
  (2 shorter events, 0.0 us)
Async XLA Ops:
  6.5 61.0 %copy-start = (bf16[768,1536]{1,0:T(8,128)(2,1)S(1)}, bf16[768,1536]{1,0:T(8,128)(2,1)}, u32[]{:S(2)}) copy-start(bf16[768,1536]{1,0:T(8,128)(2,1)} %param.9) | copy-start | bytes 7077892
  6.5 61.0 %all-gather.4.cloned.1.call-start = ((), (), s32[]{:S(2)}) async-start(), calls=%async_computation.3 | async-start | bytes 3342336 | tf_op jit(solution)/shard_map/all_gather | solution.py:39
  34.7 141.4 %reduce-scatter.6.cloned.1.call-start = ((), (), s32[]{:S(2)}) async-start(), calls=%async_computation.6 | async-start | bytes 7077888 | tf_op jit(solution)/shard_map/reduce_scatter | solution.py:53
  76.4 191.0 %reduce-scatter.4.cloned.1.call-start = ((), (), s32[]{:S(2)}) async-start(), calls=%async_computation.4 | async-start | bytes 5308416 | tf_op jit(solution)/shard_map/reduce_scatter | solution.py:47
  89.2 268.5 %all-gather.8.cloned.1.call-start = ((), (), s32[]{:S(2)}) async-start(), calls=%async_computation.7 | async-start | bytes 7077888 | tf_op jit(solution)/shard_map/all_gather | solution.py:76
  178.7 231.6 %all-gather.6.cloned.1.call-start = ((), (), s32[]{:S(2)}) async-start(), calls=%async_computation.5 | async-start | bytes 1769472 | tf_op jit(solution)/shard_map/all_gather | solution.py:75
  272.5 137.8 %copy-start.2 = (bf16[384,768]{1,0:T(8,128)(2,1)S(1)}, bf16[384,768]{1,0:T(8,128)(2,1)}, u32[]{:S(2)}) copy-start(bf16[384,768]{1,0:T(8,128)(2,1)} %param.10) | copy-start | bytes 1769476
  272.5 209.0 %reduce-scatter.8.cloned.1.call-start = ((), (), s32[]{:S(2)}) async-start(), calls=%async_computation.8 | async-start | bytes 3342336 | tf_op jit(solution)/shard_map/reduce_scatter | solution.py:78
  417.1 64.5 %copy-start.1 = (bf16[128,768]{1,0:T(8,128)(2,1)S(1)}, bf16[128,768]{1,0:T(8,128)(2,1)}, u32[]{:S(2)}) copy-start(bf16[128,768]{1,0:T(8,128)(2,1)} %param.6) | copy-start | bytes 589828
Sparse Core Ops, SparseCore 0:
  34.8 32.6 all-gather.3
  76.5 99.5 reduce-scatter.5
  180.6 86.7 reduce-scatter.3
  269.6 88.1 all-gather.7
  359.8 50.4 all-gather.5
  417.2 64.3 reduce-scatter.7
where the time goes:
time: 490 us
  waiting for transfers between devices  401 us (82%)
  matrix products  37.6 us (8%)
  blocking collectives  25.1 us (5%)
  between operations  13.5 us (3%)
  other arithmetic  7.44 us (2%)
  local copies, waits for them, and re-layouts  5.16 us (1%)
    reduce_scatter x1, waiting for transfers between devices, body(): lax.psum_scatter(jnp.dot(rows_of(), qkv_weight, preferred_element_type=jn...  88.6 us
    reduce_scatter x1, waiting for transfers between devices, body(): lax.psum_scatter(jnp.dot(rows_of(), w_up, preferred_element_type=jnp.floa...  86.8 us
    all_gather x1, waiting for transfers between devices, body(): lax.all_gather(hidden, 'row', axis=0, tiled=True)  85 us
    reduce_scatter x1, waiting for transfers between devices, body(): lax.psum_scatter((jnp.dot(attended_all, w_out, preferred_element_type=jnp...  64.5 us
    all_gather x1, waiting for transfers between devices, body(): lax.all_gather(attended, 'row', axis=0, tiled=True)  43.1 us
    all_gather x1, waiting for transfers between devices, body(): gathered = lax.all_gather(normed, 'col', axis=0, tiled=True)  32.8 us
    psum x1, blocking collectives, body(): linear_sum, square_sum = lax.psum((linear_sum, square_sum), 'row')  25.1 us
  transfers between devices with their start and end apart: 6, of which 6 were waited for; matrix products, arithmetic and copies ran while one was open for 6% of the time, Pallas kernels for 0%

commit v1 on v0

v1 whole, which is shorter than its diff:
```python
import jax
import jax.numpy as jnp
from jax import lax
from jax.experimental import pallas as pl
from jax.experimental.pallas import tpu as pltpu
from jax.sharding import PartitionSpec as P

D = 6144
HD = 128
KB = 768
EPS = 1e-06
F32 = jnp.float32
BF16 = jnp.bfloat16
MESH = pl.DeviceIdType.MESH
N_UP = 3
UP_W = 256
N_MSG = 160
N_LOC = 24


def head_norm(v):
    average = jnp.mean(v, axis=-1, keepdims=True)
    square = jnp.mean(v * v, axis=-1, keepdims=True)
    return ((v - average) * lax.rsqrt(square - average * average + EPS)).astype(BF16)


def attend(qkv):
    q = head_norm(qkv[:, 0:HD])
    k = head_norm(qkv[:, HD : 2 * HD])
    v = qkv[:, 2 * HD : 3 * HD].astype(BF16)
    scores = lax.dot_general(q, k, (((1,), (1,)), ((), ())), preferred_element_type=F32) * HD ** (-0.5)
    weights = jnp.exp(scores)
    probabilities = (weights / jnp.sum(weights, axis=-1, keepdims=True)).astype(BF16)
    return jnp.dot(probabilities, v, preferred_element_type=F32).astype(BF16)


class Ring:
    def __init__(self, send, pos, right, left, piece, a_left, a_right, b_left, b_right):
        self.send, self.right, self.left, self.piece = send, right, left, piece
        self.pos = pos
        self.plus, self.minus, self.anti = (pos + 1) % 4, (pos + 3) % 4, (pos + 2) % 4
        self.a_left, self.a_right, self.b_left, self.b_right = a_left, a_right, b_left, b_right

    def first(self):
        self.ma_r = self.send(self.piece(self.anti, 0), self.a_left, self.right)
        self.ma_l = self.send(self.piece(self.anti, 1), self.a_right, self.left)

    def second(self):
        self.mb_r1 = self.send(self.piece(self.plus, 1), self.b_left[1], self.right)
        self.mb_l0 = self.send(self.piece(self.minus, 0), self.b_right[0], self.left)

    def third(self):
        self.ma_r.wait_recv()
        mine = self.piece(self.plus, 0)
        mine[...] = (mine[...].astype(F32) + self.a_left[...].astype(F32)).astype(BF16)
        self.mb_r0 = self.send(mine, self.b_left[0], self.right)
        self.ma_l.wait_recv()
        mine = self.piece(self.minus, 1)
        mine[...] = (mine[...].astype(F32) + self.a_right[...].astype(F32)).astype(BF16)
        self.mb_l1 = self.send(mine, self.b_right[1], self.left)

    def arrive(self):
        for message in (self.mb_r1, self.mb_l0, self.mb_r0, self.mb_l1):
            message.wait_recv()

    def total(self, half):
        return (
            self.piece(self.pos, half)[...].astype(F32)
            + self.b_left[half][...].astype(F32)
            + self.b_right[half][...].astype(F32)
        )


def kernel(
    tok, gain, wq, wu, wo, wd, out,
    X, W1F, W1S, W1U, W2F, W2S, W2U,
    PF, PS, PU, AF, AS, AU, BF, BS, BU, HF, HS, HU,
    acc, OS, OC, YA0, YB0, OZ, ZA0, ZB0, ZA1, ZB1, OY, YA1, YB1,
    stats, send_sem, recv_sem, loc_sem,
):
    row, col = lax.axis_index("row"), lax.axis_index("col")
    x, zh = row // 2, row % 2
    y, zl, c = col // 4, (col // 2) % 2, col % 2
    z = zh * 2 + zl

    def dev(x_, y_, z_, c_):
        return (x_ * 2 + z_ // 2, y_ * 4 + (z_ % 2) * 2 + c_)

    xr, xl = dev((x + 1) % 4, y, z, c), dev((x + 3) % 4, y, z, c)
    yr, yl = dev(x, (y + 1) % 4, z, c), dev(x, (y + 3) % 4, z, c)
    zr, zlft = dev(x, y, (z + 1) % 4, c), dev(x, y, (z + 3) % 4, c)
    zp = dev(x, y, (z + 2) % 4, c)
    sib = dev(x, y, z, 1 - c)
    row_others = [(lax.rem(row + i, 8), col) for i in range(1, 8)]

    barrier = pltpu.get_barrier_semaphore()
    everyone = row_others + [yr, yl, zr, zlft, sib]
    for who in everyone:
        pl.semaphore_signal(barrier, inc=1, device_id=who, device_id_type=MESH)

    used = [0, 0]
    sent = []

    def send(src, dst, who):
        i = used[0]
        used[0] += 1
        copy = pltpu.make_async_remote_copy(
            src_ref=src, dst_ref=dst, send_sem=send_sem.at[i], recv_sem=recv_sem.at[i],
            device_id=who, device_id_type=MESH,
        )
        copy.start()
        sent.append(copy)
        return copy

    def local(src, dst):
        i = used[1]
        used[1] += 1
        copy = pltpu.make_async_copy(src, dst, loc_sem.at[i])
        copy.start()
        return copy

    def part(n, where):
        return pl.ds(pl.multiple_of(where * n, n), n)

    zo = 1 - zh
    own_k = part(KB, zh)

    def w1_full(who):
        return [(wq.at[j, :, part(HD, 2 * who)], W1F.at[own_k, pl.ds(j * HD, HD)]) for j in range(3)]

    w1_shared = [(wq.at[j, :, pl.ds(HD, HD)], W1S.at[own_k, pl.ds(j * HD, HD)]) for j in range(3)]

    def w1_up(who, k):
        start = pl.multiple_of(who * KB + k * UP_W, UP_W)
        return [(wu.at[:, pl.ds(start, UP_W)], W1U.at[k, own_k])]

    def w2_all(who):
        return [
            (wo.at[part(HD, 2 * who)], W2F.at[:, own_k]),
            (wo.at[pl.ds(HD, HD)], W2S.at[:, own_k]),
        ] + [
            (wd.at[pl.ds(pl.multiple_of(who * KB + k * UP_W, UP_W), UP_W)], W2U.at[k, :, own_k])
            for k in range(N_UP)
        ]

    mine_w1 = [[local(*p) for p in w1_full(zh)], [local(*p) for p in w1_shared]]
    mine_w1 += [[local(*p) for p in w1_up(zh, k)] for k in range(N_UP)]
    mine_w2 = [local(*p) for p in w2_all(zh)]

    values = tok[...].astype(F32)
    sums = [jnp.sum(values, axis=-1, keepdims=True), jnp.sum(values * values, axis=-1, keepdims=True)]
    for i, s in enumerate(sums):
        stats[0, 8 * i : 8 * i + 8] = jnp.transpose(jnp.broadcast_to(s, (128, 128)))[0:8]
    pl.semaphore_wait(barrier, len(everyone))
    moments = [send(stats.at[0], stats.at[i + 1], who) for i, who in enumerate(row_others)]
    partner_w1 = [[send(*p, zp) for p in w1_full(zo)]]
    for m in moments:
        m.wait_recv()
    all_sums = jnp.sum(stats[...], axis=0) / D
    average, square = all_sums[0:1], all_sums[8:9]
    scale = lax.rsqrt(square - average * average + EPS)
    average = jnp.transpose(jnp.broadcast_to(average, (128, 128)))[:, 0:1]
    scale = jnp.transpose(jnp.broadcast_to(scale, (128, 128)))[:, 0:1]
    X[y, zl, c, :, own_k] = ((values - average) * scale * gain[...]).astype(BF16)

    own = X.at[y, zl, c, :, own_k]
    z_msgs = {1: send(own, own, zr), 3: send(own, own, zlft), 2: send(own, own, zp)}

    def x_piece(y_, step):
        z_ = (z + step) % 4
        return X.at[y_, z_ % 2, c, :, part(KB, z_ // 2)]

    y_r, y_l = {}, {}
    for step in (0, 3, 1, 2):
        if step:
            z_msgs[{3: 1, 1: 3, 2: 2}[step]].wait_recv()
        y_r[step] = send(x_piece(y, step), x_piece(y, step), yr)
        y_l[step] = send(x_piece(y, step), x_piece(y, step), yl)
    partner_w1.append([send(*p, zp) for p in w1_shared])
    for k in range(N_UP):
        partner_w1.append([send(*p, zp) for p in w1_up(zo, k)])
    core_msgs = [send(X.at[y, :, c], X.at[y, :, c], sib)]
    yp, ym, ya = (y + 1) % 4, (y + 3) % 4, (y + 2) % 4
    fwd = []
    for step in (0, 3):
        y_r[step].wait_recv()
        fwd.append(send(x_piece(ym, step), x_piece(ym, step), yr))
    for step in (1, 2):
        y_l[step].wait_recv()
        fwd.append(send(x_piece(yp, step), x_piece(yp, step), yl))
    for step in (1, 2):
        y_r[step].wait_recv()
    core_msgs.append(send(X.at[ym, :, c], X.at[ym, :, c], sib))
    for step in (0, 3):
        y_l[step].wait_recv()
    core_msgs.append(send(X.at[yp, :, c], X.at[yp, :, c], sib))
    for m in fwd:
        m.wait_recv()
    core_msgs.append(send(X.at[ya, :, c], X.at[ya, :, c], sib))
    for m in core_msgs:
        m.wait_recv()

    def chunk(kind, k=0):
        if kind == "full":
            p, a, b, h, w1, w2, rows = PF, AF, BF, HF, W1F, W2F, 512
        elif kind == "shared":
            p, a, b, h, w1, w2, rows = PS, AS, BS, HS, W1S, W2S, 256
        else:
            p, a, b, h, w1, w2, rows = PU.at[k], AU.at[k], BU.at[k], HU.at[k], W1U.at[k], W2U.at[k], 512
        half = rows // 2

        def piece(i, which):
            return p.at[i, pl.ds(which * half, half)]

        ring = Ring(
            send, x, xr, xl, piece, a.at[0], a.at[1],
            [b.at[0, pl.ds(w * half, half)] for w in range(2)],
            [b.at[1, pl.ds(w * half, half)] for w in range(2)],
        )
        return dict(kind=kind, k=k, p=p, h=h, w1=w1, w2=w2, rows=rows, half=half, ring=ring)

    chunks = [chunk("full"), chunk("shared")] + [chunk("up", k) for k in range(N_UP)]

    def product(ch, d):
        if ch["kind"] == "shared":
            lhs = X[d, zh].reshape(256, 2 * KB)
        else:
            lhs = X[d].reshape(512, 2 * KB)
        ch["p"][d] = jnp.dot(lhs, ch["w1"][...], preferred_element_type=F32).astype(BF16)

    def stage1(ch, index):
        for copy in mine_w1[index]:
            copy.wait()
        for copy in partner_w1[index]:
            copy.wait_recv()
        product(ch, (x + 2) % 4)
        ch["ring"].first()

        def other(i, carry):
            product(ch, (x + 1 + 2 * i + i // 2 * 3) % 4)
            return carry

        lax.fori_loop(0, 3, other, 0)
        ch["ring"].second()

    def stage2(ch):
        ch["ring"].third()

    def stage3(ch):
        ring, h, half = ch["ring"], ch["h"], ch["half"]
        ring.arrive()
        if ch["kind"] == "up":
            for w in range(2):
                h[x, w * half : (w + 1) * half] = jax.nn.gelu(ring.total(w), approximate=True).astype(BF16)
        elif ch["kind"] == "full":
            for w in range(2):
                h[x, w * half : (w + 1) * half] = attend(ring.total(w))
        else:
            h[x] = attend(jnp.concatenate([ring.total(0), ring.total(1)], axis=0))
        ch["g_r"] = send(h.at[x], h.at[x], xr)
        ch["g_l"] = send(h.at[x], h.at[x], xl)

    def stage4(ch):
        h, half = ch["h"], ch["half"]
        ch["g_r"].wait_recv()
        low = h.at[(x + 3) % 4, pl.ds(0, half)]
        ch["f_r"] = send(low, low, xr)
        ch["g_l"].wait_recv()
        high = h.at[(x + 1) % 4, pl.ds(half, half)]
        ch["f_l"] = send(high, high, xl)

    def stage5(ch, first):
        ch["f_r"].wait_recv()
        ch["f_l"].wait_recv()
        h, w2 = ch["h"], ch["w2"]

        def tile(i, carry):
            d, n = i // 3, i % 3
            columns = part(512, n)
            term = jnp.dot(h[d], w2[:, columns], preferred_element_type=F32)
            if ch["kind"] == "shared":
                term = term.reshape(2, 128, 512)
                acc[d, zh, :, :, columns] += term
            else:
                term = term.reshape(2, 2, 128, 512)
                if first:
                    acc[d, :, :, :, columns] = term
                else:
                    acc[d, :, :, :, columns] += term
            return carry

        lax.fori_loop(0, 12, tile, 0)

    n = len(chunks)
    partner_w2 = []
    for t in range(n + 4):
        if t < n:
            stage1(chunks[t], t)
        if t == 2:
            partner_w2 = [send(*p, zp) for p in w2_all(zo)]
        if 0 <= t - 1 < n:
            stage2(chunks[t - 1])
        if 0 <= t - 2 < n:
            stage3(chunks[t - 2])
        if 0 <= t - 3 < n:
            stage4(chunks[t - 3])
        if 0 <= t - 4 < n:
            if t == 4:
                for copy in mine_w2:
                    copy.wait()
                for copy in partner_w2:
                    copy.wait_recv()
            stage5(chunks[t - 4], t == 4)

    def columns_of(path, which):
        return pl.ds(which * KB + path * 384, 384)

    core_out = []
    for path in range(2):

        def cast(i, carry, path=path):
            for which in range(2):
                OS[path, i // 2, i % 2, :, which * 384 : (which + 1) * 384] = acc[
                    i // 2, i % 2, 1 - c, :, columns_of(path, which)
                ].astype(BF16)
            return carry

        lax.fori_loop(0, 8, cast, 0)
        core_out.append(send(OS.at[path], OC.at[path], sib))

    rings = []
    for path in range(2):
        core_out[path].wait_recv()

        def add(i, carry, path=path):
            for which in range(2):
                there = (path, i // 2, i % 2, slice(None), slice(which * 384, (which + 1) * 384))
                OC[there] = (
                    OC[there].astype(F32) + acc[i // 2, i % 2, c, :, columns_of(path, which)]
                ).astype(BF16)
            return carry

        lax.fori_loop(0, 8, add, 0)
        if path == 0:

            def piece0(i, which):
                return OC.at[0, i, which]

            ring = Ring(send, y, yr, yl, piece0, YA0.at[0], YA0.at[1],
                        [YB0.at[0, w] for w in range(2)], [YB0.at[1, w] for w in range(2)])
        else:

            def piece1(i, which):
                return OC.at[1, pl.ds(which * 2, 2), i % 2, :, part(384, i // 2)]

            ring = Ring(send, z, zr, zlft, piece1, ZA1.at[0], ZA1.at[1],
                        [ZB1.at[0, w] for w in range(2)], [ZB1.at[1, w] for w in range(2)])
        ring.first()
        ring.second()
        rings.append(ring)
    for ring in rings:
        ring.third()
    rings[0].arrive()
    for w in range(2):
        OZ[w] = rings[0].total(w).astype(BF16)

    def piece2(i, which):
        return OZ.at[i % 2, pl.ds(which * 64, 64), part(384, i // 2)]

    last0 = Ring(send, z, zr, zlft, piece2, ZA0.at[0], ZA0.at[1],
                 [ZB0.at[0, w] for w in range(2)], [ZB0.at[1, w] for w in range(2)])
    last0.first()
    last0.second()
    rings[1].arrive()
    for w in range(2):
        OY[2 * w : 2 * w + 2] = rings[1].total(w).astype(BF16)

    def piece3(i, which):
        return OY.at[i, pl.ds(which * 64, 64)]

    last1 = Ring(send, y, yr, yl, piece3, YA1.at[0], YA1.at[1],
                 [YB1.at[0, w] for w in range(2)], [YB1.at[1, w] for w in range(2)])
    last1.first()
    last1.second()
    last0.third()
    last1.third()
    for path, last in enumerate((last0, last1)):
        last.arrive()
        for w in range(2):
            rows, columns = slice(64 * w, 64 * w + 64), slice(384 * path, 384 * path + 384)
            out[rows, columns] = (tok[rows, columns].astype(F32) + last.total(w)).astype(BF16)
    for copy in sent:
        copy.wait_send()


def vm(*shape, dtype=BF16):
    return pltpu.VMEM(shape, dtype)


def body(tokens, ln_gain, w_qkv, w_up, w_out, w_down):
    scratch = [
        vm(4, 2, 2, 128, 1536), vm(1536, 384), vm(1536, 384), vm(N_UP, 1536, UP_W),
        vm(128, 1536), vm(128, 1536), vm(N_UP, UP_W, 1536),
        vm(4, 512, 384), vm(4, 256, 384), vm(N_UP, 4, 512, UP_W),
        vm(2, 256, 384), vm(2, 128, 384), vm(N_UP, 2, 256, UP_W),
        vm(2, 512, 384), vm(2, 256, 384), vm(N_UP, 2, 512, UP_W),
        vm(4, 512, 128), vm(4, 256, 128), vm(N_UP, 4, 512, UP_W),
        vm(4, 2, 2, 128, 1536, dtype=F32),
        vm(2, 4, 2, 128, 768), vm(2, 4, 2, 128, 768),
        vm(2, 128, 768), vm(2, 2, 128, 768), vm(2, 128, 768), vm(2, 64, 384), vm(2, 2, 64, 384),
        vm(2, 2, 128, 384), vm(2, 2, 2, 128, 384), vm(4, 128, 384), vm(2, 64, 384), vm(2, 2, 64, 384),
        vm(8, 16, 128, dtype=F32),
        pltpu.SemaphoreType.DMA((N_MSG,)), pltpu.SemaphoreType.DMA((N_MSG,)), pltpu.SemaphoreType.DMA((N_LOC,)),
    ]
    vmem, anywhere = pl.BlockSpec(memory_space=pltpu.VMEM), pl.BlockSpec(memory_space=pl.ANY)
    return pl.pallas_call(
        kernel,
        out_shape=jax.ShapeDtypeStruct((128, KB), BF16),
        in_specs=[vmem, vmem, anywhere, anywhere, anywhere, anywhere],
        out_specs=vmem,
        scratch_shapes=scratch,
        compiler_params=pltpu.CompilerParams(
            collective_id=0, has_side_effects=True, vmem_limit_bytes=62 << 20
        ),
        name="layer",
    )(tokens, ln_gain.reshape(1, KB), jnp.transpose(w_qkv, (1, 0, 2)), w_up, w_out, w_down)


def solution(mesh):
    return jax.shard_map(
        body,
        mesh=mesh,
        in_specs=(
            P("col", "row"),
            P("row"),
            P("row", None, "col"),
            P("row", "col"),
            P("col", "row"),
            P("col", "row"),
        ),
        out_specs=P("col", "row"),
        check_vma=False,
    )
```

time: 490 us -> 171 us (0.35)
  waiting for transfers between devices: 401 us -> 0 us
  Pallas kernels: 0 us -> 166 us
  matrix products: 37.6 us -> 0 us
  blocking collectives: 25.1 us -> 0 us
  between operations: 13.5 us -> 0.01 us
  other arithmetic: 7.44 us -> 0 us
    reduce_scatter x3 -> x0, waiting for transfers between devices: 240 us -> none  [the longest x1 88.6 us: body(): lax.psum_scatter(jnp.dot(rows_of(), qkv_weight, preferred_element_type=jn...]
    pallas_call x0 -> x1, Pallas kernels: none -> 166 us  [body(): pl.pallas_call(kernel, out_shape=jax.ShapeDtypeStruct((128, KB), BF16), i...]
    all_gather x3 -> x0, waiting for transfers between devices: 161 us -> none  [the longest x1 85 us: body(): lax.all_gather(hidden, 'row', axis=0, tiled=True)]
    dot_general x6 -> x0, matrix products: 37.6 us -> none  [the longest x1 9.46 us: body(): jnp.dot(hidden_all, w_down, preferred_element_type=jnp.float32)]
    psum x1 -> x0, blocking collectives: 25.1 us -> none  [body(): linear_sum, square_sum = lax.psum((linear_sum, square_sum), 'row')]
    convert_element_type x3 -> x0, other arithmetic: 6 us -> none  [the longest x1 2.57 us: body(): hidden = jax.nn.gelu(up_sum, approximate=True).astype(jnp.bfloat16)]
  transfers between devices with their start and end apart: 6 -> 0, of which waited for: 6 -> 0; matrix products, arithmetic and copies ran while one was open for 6% -> 0% of each run, Pallas kernels for 0% -> 0%
where the time goes in v1:
time: 171 us; the launch traced here: 169 us
  Pallas kernels  166 us (97%)
  local copies, waits for them, and re-layouts  2.88 us (2%)
    pallas_call x1, Pallas kernels, body(): pl.pallas_call(kernel, out_shape=jax.ShapeDtypeStruct((128, KB), BF16), i...  166 us

profile of v1, /device:TPU:0, one launch (start us, length us, event | category | flops | bytes accessed | tf_op | source)
XLA Modules:
  0.0 169.1 jit_solution(11363850419876053357)
XLA Ops:
  0.0 1.3 reshape.3.gain
  1.3 166.2 %layer.1 = bf16[128,768]{1,0:T(8,128)(2,1)} custom-call(bf16[128,768]{1,0:T(8,128)(2,1)} %tok.1, f32[1,768]{1,0:T(1,128)} %reshape.3.gain, bf16[3,768,384]{2,1,0:T(8,128)(2,1)} %bitcast.1, bf16[768,1536]{1,0:T(8,128)(2,1)} %wu.1, bf16[384,768]{1,0:T(8,128)(2,1)} %wo.1, bf16[1536,768]{1,0:T(8,128)(2,1)} %wd.1), custom_call_target="tpu_custom_call" | custom-call | tf_op jit(solution)/shard_map/layer/pallas_call | solution.py:416
  167.5 1.6 copy.8

commit v2 on v1

v2 whole, which is shorter than its diff:
```python
import jax
import jax.numpy as jnp
from jax import lax
from jax.experimental import pallas as pl
from jax.experimental.pallas import tpu as pltpu
from jax.sharding import PartitionSpec as P

D = 6144
HD = 128
KB = 768
EPS = 1e-06
F32 = jnp.float32
BF16 = jnp.bfloat16
MESH = pl.DeviceIdType.MESH
N_UP = 3
UP_W = 256
N_MSG = 256
N_LOC = 24


def head_norm(v):
    average = jnp.mean(v, axis=-1, keepdims=True)
    square = jnp.mean(v * v, axis=-1, keepdims=True)
    return ((v - average) * lax.rsqrt(square - average * average + EPS)).astype(BF16)


def attend(qkv):
    q = head_norm(qkv[:, 0:HD])
    k = head_norm(qkv[:, HD : 2 * HD])
    v = qkv[:, 2 * HD : 3 * HD].astype(BF16)
    scores = lax.dot_general(q, k, (((1,), (1,)), ((), ())), preferred_element_type=F32) * HD ** (-0.5)
    weights = jnp.exp(scores)
    probabilities = (weights / jnp.sum(weights, axis=-1, keepdims=True)).astype(BF16)
    return jnp.dot(probabilities, v, preferred_element_type=F32).astype(BF16)


class Ring:
    def __init__(self, send, pos, right, left, piece, a_left, a_right, b_left, b_right):
        self.send, self.right, self.left, self.piece = send, right, left, piece
        self.pos = pos
        self.plus, self.minus, self.anti = (pos + 1) % 4, (pos + 3) % 4, (pos + 2) % 4
        self.a_left, self.a_right, self.b_left, self.b_right = a_left, a_right, b_left, b_right

    def first(self):
        self.ma_r = self.send(self.piece(self.anti, 0), self.a_left, self.right)
        self.ma_l = self.send(self.piece(self.anti, 1), self.a_right, self.left)

    def second(self):
        self.mb_r1 = self.send(self.piece(self.plus, 1), self.b_left[1], self.right)
        self.mb_l0 = self.send(self.piece(self.minus, 0), self.b_right[0], self.left)

    def third(self):
        self.ma_r.wait_recv()
        mine = self.piece(self.plus, 0)
        mine[...] = (mine[...].astype(F32) + self.a_left[...].astype(F32)).astype(BF16)
        self.mb_r0 = self.send(mine, self.b_left[0], self.right)
        self.ma_l.wait_recv()
        mine = self.piece(self.minus, 1)
        mine[...] = (mine[...].astype(F32) + self.a_right[...].astype(F32)).astype(BF16)
        self.mb_l1 = self.send(mine, self.b_right[1], self.left)

    def arrive(self):
        for message in (self.mb_r1, self.mb_l0, self.mb_r0, self.mb_l1):
            message.wait_recv()

    def total(self, half):
        return (
            self.piece(self.pos, half)[...].astype(F32)
            + self.b_left[half][...].astype(F32)
            + self.b_right[half][...].astype(F32)
        )


N_OUT = 6


def kernel(
    tok, gain, wq, wu, wo, wd, out,
    X, W1F, W1S, W1U, W2F, W2S, W2U,
    PF, PS, PU, AF, AS, AU, BF, BS, BU, HF, HS, HU,
    acc, OS, OC, Y0A, Y0B, Z0P, Z0A, Z0B, Z1A, Z1B, Y1P, Y1A, Y1B,
    stats, send_sem, recv_sem, loc_sem,
):
    row, col = lax.axis_index("row"), lax.axis_index("col")
    x, zh = row // 2, row % 2
    y, zl, c = col // 4, (col // 2) % 2, col % 2
    z = zh * 2 + zl

    def dev(x_, y_, z_, c_):
        return (x_ * 2 + z_ // 2, y_ * 4 + (z_ % 2) * 2 + c_)

    xr, xl, xa = dev((x + 1) % 4, y, z, c), dev((x + 3) % 4, y, z, c), dev((x + 2) % 4, y, z, c)
    yr, yl = dev(x, (y + 1) % 4, z, c), dev(x, (y + 3) % 4, z, c)
    zr, zlft = dev(x, y, (z + 1) % 4, c), dev(x, y, (z + 3) % 4, c)
    zp = dev(x, y, (z + 2) % 4, c)
    sib = dev(x, y, z, 1 - c)

    barrier = pltpu.get_barrier_semaphore()
    everyone = [xa, zp, xr, xl, yr, yl, zr, zlft, sib]
    for who in everyone:
        pl.semaphore_signal(barrier, inc=1, device_id=who, device_id_type=MESH)

    used = [0, 0]
    sent = []

    def send(src, dst, who):
        i = used[0]
        used[0] += 1
        copy = pltpu.make_async_remote_copy(
            src_ref=src, dst_ref=dst, send_sem=send_sem.at[i], recv_sem=recv_sem.at[i],
            device_id=who, device_id_type=MESH,
        )
        copy.start()
        sent.append(copy)
        return copy

    def local(src, dst):
        i = used[1]
        used[1] += 1
        copy = pltpu.make_async_copy(src, dst, loc_sem.at[i])
        copy.start()
        return copy

    def part(n, where):
        return pl.ds(pl.multiple_of(where * n, n), n)

    zo = 1 - zh
    own_k = part(KB, zh)

    values = tok[...].astype(F32)
    sums = [jnp.sum(values, axis=-1, keepdims=True), jnp.sum(values * values, axis=-1, keepdims=True)]
    for i, s in enumerate(sums):
        stats[0, 8 * i : 8 * i + 8] = jnp.transpose(jnp.broadcast_to(s, (128, 128)))[0:8]
    pl.semaphore_wait(barrier, len(everyone))
    send(stats.at[0], stats.at[1], zp).wait_recv()
    stats[2] = stats[0] + stats[1]
    moments = [send(stats.at[2], stats.at[3 + i], who) for i, who in enumerate((xr, xl, xa))]

    def w1_full(who):
        return [(wq.at[j, :, part(HD, 2 * who)], W1F.at[own_k, pl.ds(j * HD, HD)]) for j in range(3)]

    w1_shared = [(wq.at[j, :, pl.ds(HD, HD)], W1S.at[own_k, pl.ds(j * HD, HD)]) for j in range(3)]

    def up_part(who, k):
        return pl.ds(pl.multiple_of(who * KB + k * UP_W, UP_W), UP_W)

    def w1_parts(who):
        parts = [[(wu.at[:, up_part(who, k)], W1U.at[k, own_k])] for k in range(N_UP)]
        return parts + [w1_full(who), w1_shared]

    def w2_parts(who):
        parts = [[(wd.at[up_part(who, k)], W2U.at[k, :, own_k])] for k in range(N_UP)]
        return parts + [
            [(wo.at[part(HD, 2 * who)], W2F.at[:, own_k])],
            [(wo.at[pl.ds(HD, HD)], W2S.at[:, own_k])],
        ]

    mine_w1 = [[local(*p) for p in ps] for ps in w1_parts(zh)]
    mine_w2 = [[local(*p) for p in ps] for ps in w2_parts(zh)]
    for m in moments:
        m.wait_recv()
    all_sums = (stats[2] + stats[3] + stats[4] + stats[5]) / D
    average, square = all_sums[0:1], all_sums[8:9]
    scale = lax.rsqrt(square - average * average + EPS)
    average = jnp.transpose(jnp.broadcast_to(average, (128, 128)))[:, 0:1]
    scale = jnp.transpose(jnp.broadcast_to(scale, (128, 128)))[:, 0:1]
    X[y, zl, c, :, own_k] = ((values - average) * scale * gain[...].reshape(1, KB)).astype(BF16)

    own = X.at[y, zl, c, :, own_k]
    z_msgs = {3: send(own, own, zr), 1: send(own, own, zlft), 2: send(own, own, zp)}
    partner_w1 = [[send(*p, zp) for p in ps] for ps in w1_parts(zo)]
    partner_w2 = [[send(*p, zp) for p in ps] for ps in w2_parts(zo)]

    def x_piece(y_, step):
        z_ = (z + step) % 4
        return X.at[y_, z_ % 2, c, :, part(KB, z_ // 2)]

    yp, ym, ya = (y + 1) % 4, (y + 3) % 4, (y + 2) % 4
    y_r, y_l, core_msgs, fwd = {}, {}, {}, []
    for step in (0, 3, 1, 2):
        if step:
            z_msgs[step].wait_recv()
        y_r[step] = send(x_piece(y, step), x_piece(y, step), yr)
        y_l[step] = send(x_piece(y, step), x_piece(y, step), yl)
    core_msgs[0] = send(X.at[y, :, c], X.at[y, :, c], sib)

    def gather_forward():
        for step in (0, 3):
            y_r[step].wait_recv()
            fwd.append(send(x_piece(ym, step), x_piece(ym, step), yr))
        for step in (1, 2):
            y_l[step].wait_recv()
            fwd.append(send(x_piece(yp, step), x_piece(yp, step), yl))

    def gather_near():
        for step in (1, 2):
            y_r[step].wait_recv()
        core_msgs[2] = send(X.at[ym, :, c], X.at[ym, :, c], sib)
        for step in (0, 3):
            y_l[step].wait_recv()
        core_msgs[1] = send(X.at[yp, :, c], X.at[yp, :, c], sib)
        for i in (2, 1):
            core_msgs[i].wait_recv()

    def gather_far():
        for m in fwd:
            m.wait_recv()
        core_msgs[3] = send(X.at[ya, :, c], X.at[ya, :, c], sib)
        core_msgs[3].wait_recv()

    def unit(kind, k, group=None):
        if kind == "full":
            p, a, b, h = PF, AF, BF, HF
        elif kind == "shared":
            p, a, b, h = PS, AS, BS, HS
        else:
            p, a, b, h = PU.at[k], AU.at[k], BU.at[k], HU.at[k]
        rows = {"full": 256, "shared": 128}.get(kind)
        blocks = None

        def at(half=None):
            if rows:
                return () if half is None else (pl.ds(rows * half, rows),)
            if group is None:
                return () if half is None else (pl.ds(2 * half, 2),)
            if group == 1:
                return (pl.ds(1, 2),) if half is None else (1 + half,)
            return (blocks[0],) if half is None else (blocks[0], pl.ds(64 * half, 64))

        if kind == "up":
            blocks = {None: (0, 1, 2, 3), 0: (0,), 1: (1, 2), 2: (3,)}[group]
        if rows or group is None:
            a_l, a_r = a.at[0], a.at[1]
        elif group == 1:
            a_l, a_r = a.at[0, 1], a.at[1, 1]
        else:
            a_l, a_r = (a.at[side, 0, pl.ds(32 * group, 64)] for side in range(2))
        ring = Ring(
            send, x, xr, xl, lambda i, half: p.at[(i, *at(half))], a_l, a_r,
            [b.at[(0, *at(half))] for half in range(2)], [b.at[(1, *at(half))] for half in range(2)],
        )
        return dict(kind=kind, k=k, p=p, h=h, at=at, blocks=blocks, ring=ring)

    def columns_ready(parts, partner, k):
        for copy in parts[k]:
            copy.wait()
        for copy in partner[k]:
            copy.wait_recv()
        parts[k], partner[k] = [], []

    def produce(u):
        columns_ready(mine_w1, partner_w1, u["k"])
        kind, ring, p = u["kind"], u["ring"], u["p"]
        if kind == "up":
            w1, blocks = W1U.at[u["k"]], u["blocks"]

            def one(i, carry):
                beta = blocks[0] + i
                b = (y + beta + beta // 2 - 2 * (beta // 3)) % 4
                term = jnp.dot(X[b].reshape(512, 2 * KB), w1[...], preferred_element_type=F32)
                p[:, beta] = term.reshape(4, 128, UP_W).astype(BF16)
                return carry

            lax.fori_loop(0, len(blocks), one, 0)
            ring.first()
            ring.second()
            return

        def place(d):
            if kind == "shared":
                lhs, w1 = X[d, zh].reshape(256, 2 * KB), W1S
            else:
                lhs, w1 = X[d].reshape(512, 2 * KB), W1F
            p[d] = jnp.dot(lhs, w1[...], preferred_element_type=F32).astype(BF16)

        place((x + 2) % 4)
        ring.first()

        def other(i, carry):
            place((x + 1 + 2 * i + i // 2 * 3) % 4)
            return carry

        lax.fori_loop(0, 3, other, 0)
        ring.second()

    def combine(u):
        u["ring"].third()

    def activate(u):
        kind, ring, h, at = u["kind"], u["ring"], u["h"], u["at"]
        ring.arrive()
        if kind == "up":
            for half in range(2):
                h[(x, *at(half))] = jax.nn.gelu(ring.total(half), approximate=True).astype(BF16)
        elif kind == "full":
            for half in range(2):
                h[(x, *at(half))] = attend(ring.total(half))
        else:
            h[x] = attend(jnp.concatenate([ring.total(0), ring.total(1)], axis=0))
        mine = h.at[(x, *at())]
        u["g_r"] = send(mine, mine, xr)
        u["g_l"] = send(mine, mine, xl)

    def forward(u):
        h, at = u["h"], u["at"]
        u["g_r"].wait_recv()
        low = h.at[((x + 3) % 4, *at(0))]
        u["f_r"] = send(low, low, xr)
        u["g_l"].wait_recv()
        high = h.at[((x + 1) % 4, *at(1))]
        u["f_l"] = send(high, high, xl)

    def landed(*units):
        for u in units:
            u["f_r"].wait_recv()
            u["f_l"].wait_recv()

    def out_columns(w2, s):
        return jnp.concatenate([w2[:, part(128, s)], w2[:, pl.ds(pl.multiple_of(KB + s * 128, 128), 128)]], axis=1)

    def finish_up(k):
        columns_ready(mine_w2, partner_w2, k)
        h, w2 = HU.at[k], W2U.at[k]

        def tile(i, carry):
            beta, s = i // N_OUT, i % N_OUT
            b = (y + beta + beta // 2 - 2 * (beta // 3)) % 4
            term = jnp.dot(h[:, beta].reshape(512, UP_W), out_columns(w2, s), preferred_element_type=F32)
            term = term.reshape(2, 2, 128, 256)
            if k == 0:
                acc[s, b] = term
            else:
                acc[s, b] += term
            return carry

        lax.fori_loop(0, 4 * N_OUT, tile, 0)

    def finish_full():
        columns_ready(mine_w2, partner_w2, 3)

        def tile(i, carry):
            d, s = i // N_OUT, i % N_OUT
            term = jnp.dot(HF[d], out_columns(W2F, s), preferred_element_type=F32)
            acc[s, d] += term.reshape(2, 2, 128, 256)
            return carry

        lax.fori_loop(0, 4 * N_OUT, tile, 0)

    near = [unit("up", k, 0) for k in range(2)]
    middle = [unit("up", k, 1) for k in range(2)]
    far = [unit("up", k, 2) for k in range(2)]
    whole = unit("up", 2)
    full, shared = unit("full", 3), unit("shared", 4)

    core_msgs[0].wait_recv()
    produce(near[0])
    combine(near[0])
    gather_forward()
    produce(near[1])
    activate(near[0])
    combine(near[1])
    gather_near()
    produce(middle[0])
    produce(middle[1])
    forward(near[0])
    activate(near[1])
    combine(middle[0])
    combine(middle[1])
    gather_far()
    produce(far[0])
    produce(far[1])
    forward(near[1])
    activate(middle[0])
    combine(far[0])
    activate(middle[1])
    combine(far[1])
    produce(whole)
    activate(far[0])
    activate(far[1])
    forward(middle[0])
    forward(middle[1])
    combine(whole)
    produce(full)
    forward(far[0])
    forward(far[1])
    activate(whole)
    combine(full)
    produce(shared)
    forward(whole)
    activate(full)
    combine(shared)
    landed(near[0], middle[0], far[0])
    finish_up(0)
    forward(full)
    activate(shared)
    landed(near[1], middle[1], far[1])
    finish_up(1)
    forward(shared)
    landed(whole)
    finish_up(2)
    landed(full)
    finish_full()
    landed(shared)
    columns_ready(mine_w2, partner_w2, 4)

    def out_core(s):
        columns = out_columns(W2S, s)

        def one(d, carry):
            term = jnp.dot(HS[d], columns, preferred_element_type=F32)
            acc[s, d, zh] += term.reshape(2, 128, 256)
            OS[s, d] = acc[s, d, :, 1 - c].astype(BF16)
            return carry

        lax.fori_loop(0, 4, one, 0)
        return send(OS.at[s], OC.at[s], sib)

    def out_first(s, message):
        message.wait_recv()

        def one(d, carry):
            OC[s, d] = (OC[s, d].astype(F32) + acc[s, d, :, c]).astype(BF16)
            return carry

        lax.fori_loop(0, 4, one, 0)
        if s < 3:
            ring = Ring(
                send, y, yr, yl, lambda i, half: OC.at[s, i, half], Y0A.at[s, 0], Y0A.at[s, 1],
                [Y0B.at[s, 0, half] for half in range(2)], [Y0B.at[s, 1, half] for half in range(2)],
            )
        else:
            ring = Ring(
                send, z, zr, zlft,
                lambda i, half: OC.at[s, pl.ds(2 * half, 2), i % 2, :, part(128, i // 2)],
                Z1A.at[s - 3, 0], Z1A.at[s - 3, 1],
                [Z1B.at[s - 3, 0, half] for half in range(2)], [Z1B.at[s - 3, 1, half] for half in range(2)],
            )
        ring.first()
        ring.second()
        return ring

    def out_second(s, before):
        before.arrive()
        if s < 3:
            for half in range(2):
                Z0P[s, half] = before.total(half).astype(BF16)
            ring = Ring(
                send, z, zr, zlft,
                lambda i, half: Z0P.at[s, i % 2, pl.ds(64 * half, 64), part(128, i // 2)],
                Z0A.at[s, 0], Z0A.at[s, 1],
                [Z0B.at[s, 0, half] for half in range(2)], [Z0B.at[s, 1, half] for half in range(2)],
            )
        else:
            j = s - 3
            for half in range(2):
                Y1P[j, 2 * half : 2 * half + 2] = before.total(half).astype(BF16)
            ring = Ring(
                send, y, yr, yl, lambda i, half: Y1P.at[j, i, pl.ds(64 * half, 64)],
                Y1A.at[j, 0], Y1A.at[j, 1],
                [Y1B.at[j, 0, half] for half in range(2)], [Y1B.at[j, 1, half] for half in range(2)],
            )
        ring.first()
        ring.second()
        return ring

    def out_last(s, ring):
        ring.arrive()
        for half in range(2):
            rows, columns = slice(64 * half, 64 * half + 64), slice(128 * s, 128 * s + 128)
            out[rows, columns] = (tok[rows, columns].astype(F32) + ring.total(half)).astype(BF16)

    sequence = (0, 3, 1, 4, 2, 5)
    core, one, two = {}, {}, {}
    for t in range(N_OUT + 8):
        if t < N_OUT:
            core[t] = out_core(sequence[t])
        if 0 <= t - 1 < N_OUT:
            one[t - 1] = out_first(sequence[t - 1], core[t - 1])
        if 0 <= t - 3 < N_OUT:
            one[t - 3].third()
        if 0 <= t - 5 < N_OUT:
            two[t - 5] = out_second(sequence[t - 5], one[t - 5])
        if 0 <= t - 6 < N_OUT:
            two[t - 6].third()
        if 0 <= t - 8 < N_OUT:
            out_last(sequence[t - 8], two[t - 8])
    for copy in sent:
        copy.wait_send()


def vm(*shape, dtype=BF16):
    return pltpu.VMEM(shape, dtype)


def body(tokens, ln_gain, w_qkv, w_up, w_out, w_down):
    scratch = [
        vm(4, 2, 2, 128, 1536), vm(1536, 384), vm(1536, 384), vm(N_UP, 1536, UP_W),
        vm(128, 1536), vm(128, 1536), vm(N_UP, UP_W, 1536),
        vm(4, 512, 384), vm(4, 256, 384), vm(N_UP, 4, 4, 128, UP_W),
        vm(2, 256, 384), vm(2, 128, 384), vm(N_UP, 2, 2, 128, UP_W),
        vm(2, 512, 384), vm(2, 256, 384), vm(N_UP, 2, 4, 128, UP_W),
        vm(4, 512, 128), vm(4, 256, 128), vm(N_UP, 4, 4, 128, UP_W),
        vm(N_OUT, 4, 2, 2, 128, 256, dtype=F32), vm(N_OUT, 4, 2, 128, 256), vm(N_OUT, 4, 2, 128, 256),
        vm(3, 2, 128, 256), vm(3, 2, 2, 128, 256), vm(3, 2, 128, 256), vm(3, 2, 64, 128), vm(3, 2, 2, 64, 128),
        vm(3, 2, 2, 128, 128), vm(3, 2, 2, 2, 128, 128), vm(3, 4, 128, 128), vm(3, 2, 64, 128), vm(3, 2, 2, 64, 128),
        vm(8, 16, 128, dtype=F32),
        pltpu.SemaphoreType.DMA((N_MSG,)), pltpu.SemaphoreType.DMA((N_MSG,)), pltpu.SemaphoreType.DMA((N_LOC,)),
    ]
    vmem, anywhere = pl.BlockSpec(memory_space=pltpu.VMEM), pl.BlockSpec(memory_space=pl.ANY)
    return pl.pallas_call(
        kernel,
        out_shape=jax.ShapeDtypeStruct((128, KB), BF16),
        in_specs=[vmem, vmem, anywhere, anywhere, anywhere, anywhere],
        out_specs=vmem,
        scratch_shapes=scratch,
        compiler_params=pltpu.CompilerParams(
            collective_id=0, has_side_effects=True, vmem_limit_bytes=62 << 20
        ),
        name="layer",
    )(tokens, ln_gain, jnp.transpose(w_qkv, (1, 0, 2)), w_up, w_out, w_down)


def solution(mesh):
    return jax.shard_map(
        body,
        mesh=mesh,
        in_specs=(
            P("col", "row"),
            P("row"),
            P("row", None, "col"),
            P("row", "col"),
            P("col", "row"),
            P("col", "row"),
        ),
        out_specs=P("col", "row"),
        check_vma=False,
    )
```

time: 171 us -> 174 us (1.018)
  Pallas kernels: 166 us -> 171 us
    pallas_call x1, Pallas kernels: 166 us -> 171 us  [body(): pl.pallas_call(kernel, out_shape=jax.ShapeDtypeStruct((128, KB), BF16), i...]
where the time goes in v2:
time: 174 us; the launch traced here: 173 us
  Pallas kernels  171 us (98%)
    pallas_call x1, Pallas kernels, body(): pl.pallas_call(kernel, out_shape=jax.ShapeDtypeStruct((128, KB), BF16), i...  171 us

profile of v2, /device:TPU:0, one launch (start us, length us, event | category | flops | bytes accessed | tf_op | source)
XLA Modules:
  0.0 173.0 jit_solution(8945544095449598463)
XLA Ops:
  0.0 171.4 %layer.1 = bf16[128,768]{1,0:T(8,128)(2,1)} custom-call(bf16[128,768]{1,0:T(8,128)(2,1)} %tok.1, f32[768]{0:T(1024)} %gain.1, bf16[3,768,384]{2,1,0:T(8,128)(2,1)} %bitcast.1, bf16[768,1536]{1,0:T(8,128)(2,1)} %wu.1, bf16[384,768]{1,0:T(8,128)(2,1)} %wo.1, bf16[1536,768]{1,0:T(8,128)(2,1)} %wd.1), custom_call_target="tpu_custom_call" | custom-call | tf_op jit(solution)/shard_map/layer/pallas_call | solution.py:510
  171.4 1.6 copy.8

commit v3 on v2

--- a/solution.py
+++ b/solution.py
@@ -8,6 +8,7 @@
 D = 6144
 HD = 128
 KB = 768
+PATCH = 256
 EPS = 1e-06
 F32 = jnp.float32
 BF16 = jnp.bfloat16
@@ -76,7 +77,7 @@
 
 def kernel(
     tok, gain, wq, wu, wo, wd, out,
-    X, W1F, W1S, W1U, W2F, W2S, W2U,
+    X, W1F, W1S, W1U, W2,
     PF, PS, PU, AF, AS, AU, BF, BS, BU, HF, HS, HU,
     acc, OS, OC, Y0A, Y0B, Z0P, Z0A, Z0B, Z1A, Z1B, Y1P, Y1A, Y1B,
     stats, send_sem, recv_sem, loc_sem,
@@ -89,14 +90,16 @@
     def dev(x_, y_, z_, c_):
         return (x_ * 2 + z_ // 2, y_ * 4 + (z_ % 2) * 2 + c_)
 
-    xr, xl, xa = dev((x + 1) % 4, y, z, c), dev((x + 3) % 4, y, z, c), dev((x + 2) % 4, y, z, c)
+    xr, xl = dev((x + 1) % 4, y, z, c), dev((x + 3) % 4, y, z, c)
     yr, yl = dev(x, (y + 1) % 4, z, c), dev(x, (y + 3) % 4, z, c)
     zr, zlft = dev(x, y, (z + 1) % 4, c), dev(x, y, (z + 3) % 4, c)
     zp = dev(x, y, (z + 2) % 4, c)
     sib = dev(x, y, z, 1 - c)
+    zo = 1 - zh
 
     barrier = pltpu.get_barrier_semaphore()
-    everyone = [xa, zp, xr, xl, yr, yl, zr, zlft, sib]
+    row_others = [(lax.rem(row + i, 8), col) for i in range(1, 8)]
+    everyone = row_others + [yr, yl, zr, zlft, sib]
     for who in everyone:
         pl.semaphore_signal(barrier, inc=1, device_id=who, device_id_type=MESH)
 
@@ -124,7 +127,9 @@
     def part(n, where):
         return pl.ds(pl.multiple_of(where * n, n), n)
 
-    zo = 1 - zh
+    for d in range(4):
+        HS[d, zo] = jnp.zeros((PATCH, HD), BF16)
+
     own_k = part(KB, zh)
 
     values = tok[...].astype(F32)
@@ -132,9 +137,7 @@
     for i, s in enumerate(sums):
         stats[0, 8 * i : 8 * i + 8] = jnp.transpose(jnp.broadcast_to(s, (128, 128)))[0:8]
     pl.semaphore_wait(barrier, len(everyone))
-    send(stats.at[0], stats.at[1], zp).wait_recv()
-    stats[2] = stats[0] + stats[1]
-    moments = [send(stats.at[2], stats.at[3 + i], who) for i, who in enumerate((xr, xl, xa))]
+    moments = [send(stats.at[0], stats.at[i + 1], who) for i, who in enumerate(row_others)]
 
     def w1_full(who):
         return [(wq.at[j, :, part(HD, 2 * who)], W1F.at[own_k, pl.ds(j * HD, HD)]) for j in range(3)]
@@ -149,17 +152,21 @@
         return parts + [w1_full(who), w1_shared]
 
     def w2_parts(who):
-        parts = [[(wd.at[up_part(who, k)], W2U.at[k, :, own_k])] for k in range(N_UP)]
-        return parts + [
-            [(wo.at[part(HD, 2 * who)], W2F.at[:, own_k])],
-            [(wo.at[pl.ds(HD, HD)], W2S.at[:, own_k])],
+        return [
+            [(wd.at[pl.ds(pl.multiple_of(who * KB, KB), 512)], W2.at[pl.ds(0, 512), own_k])],
+            [
+                (wd.at[up_part(who, 2)], W2.at[pl.ds(512, UP_W), own_k]),
+                (wo.at[part(HD, 2 * who)], W2.at[pl.ds(768, HD), own_k]),
+                (wo.at[pl.ds(HD, HD)], W2.at[pl.ds(896, HD), own_k]),
+            ],
         ]
 
+    partner_w1 = [[send(*p, zp) for p in ps] for ps in w1_parts(zo)[:1]]
     mine_w1 = [[local(*p) for p in ps] for ps in w1_parts(zh)]
     mine_w2 = [[local(*p) for p in ps] for ps in w2_parts(zh)]
     for m in moments:
         m.wait_recv()
-    all_sums = (stats[2] + stats[3] + stats[4] + stats[5]) / D
+    all_sums = jnp.sum(stats[...], axis=0) / D
     average, square = all_sums[0:1], all_sums[8:9]
     scale = lax.rsqrt(square - average * average + EPS)
     average = jnp.transpose(jnp.broadcast_to(average, (128, 128)))[:, 0:1]
@@ -168,7 +175,7 @@
 
     own = X.at[y, zl, c, :, own_k]
     z_msgs = {3: send(own, own, zr), 1: send(own, own, zlft), 2: send(own, own, zp)}
-    partner_w1 = [[send(*p, zp) for p in ps] for ps in w1_parts(zo)]
+    partner_w1 += [[send(*p, zp) for p in ps] for ps in w1_parts(zo)[1:]]
     partner_w2 = [[send(*p, zp) for p in ps] for ps in w2_parts(zo)]
 
     def x_piece(y_, step):
@@ -216,6 +223,7 @@
         else:
             p, a, b, h = PU.at[k], AU.at[k], BU.at[k], HU.at[k]
         rows = {"full": 256, "shared": 128}.get(kind)
+        base = (zh,) if kind == "shared" else ()
         blocks = None
 
         def at(half=None):
@@ -239,7 +247,7 @@
             send, x, xr, xl, lambda i, half: p.at[(i, *at(half))], a_l, a_r,
             [b.at[(0, *at(half))] for half in range(2)], [b.at[(1, *at(half))] for half in range(2)],
         )
-        return dict(kind=kind, k=k, p=p, h=h, at=at, blocks=blocks, ring=ring)
+        return dict(kind=kind, k=k, p=p, h=h, at=at, base=base, blocks=blocks, ring=ring)
 
     def columns_ready(parts, partner, k):
         for copy in parts[k]:
@@ -256,7 +264,7 @@
 
             def one(i, carry):
                 beta = blocks[0] + i
-                b = (y + beta + beta // 2 - 2 * (beta // 3)) % 4
+                b = block_at(beta)
                 term = jnp.dot(X[b].reshape(512, 2 * KB), w1[...], preferred_element_type=F32)
                 p[:, beta] = term.reshape(4, 128, UP_W).astype(BF16)
                 return carry
@@ -296,18 +304,18 @@
             for half in range(2):
                 h[(x, *at(half))] = attend(ring.total(half))
         else:
-            h[x] = attend(jnp.concatenate([ring.total(0), ring.total(1)], axis=0))
-        mine = h.at[(x, *at())]
+            h[x, zh] = attend(jnp.concatenate([ring.total(0), ring.total(1)], axis=0))
+        mine = h.at[(x, *u["base"], *at())]
         u["g_r"] = send(mine, mine, xr)
         u["g_l"] = send(mine, mine, xl)
 
     def forward(u):
         h, at = u["h"], u["at"]
         u["g_r"].wait_recv()
-        low = h.at[((x + 3) % 4, *at(0))]
+        low = h.at[((x + 3) % 4, *u["base"], *at(0))]
         u["f_r"] = send(low, low, xr)
         u["g_l"].wait_recv()
-        high = h.at[((x + 1) % 4, *at(1))]
+        high = h.at[((x + 1) % 4, *u["base"], *at(1))]
         u["f_l"] = send(high, high, xl)
 
     def landed(*units):
@@ -315,33 +323,22 @@
             u["f_r"].wait_recv()
             u["f_l"].wait_recv()
 
-    def out_columns(w2, s):
-        return jnp.concatenate([w2[:, part(128, s)], w2[:, pl.ds(pl.multiple_of(KB + s * 128, 128), 128)]], axis=1)
-
-    def finish_up(k):
-        columns_ready(mine_w2, partner_w2, k)
-        h, w2 = HU.at[k], W2U.at[k]
+    def out_columns(first, s):
+        rows = pl.ds(first, 512)
+        left, right = part(128, s), pl.ds(pl.multiple_of(KB + s * 128, 128), 128)
+        return jnp.concatenate([W2[rows, left], W2[rows, right]], axis=1)
+
+    def block_at(beta):
+        return (y + beta + beta // 2 - 2 * (beta // 3)) % 4
+
+    def second_product():
+        columns_ready(mine_w2, partner_w2, 0)
 
         def tile(i, carry):
             beta, s = i // N_OUT, i % N_OUT
-            b = (y + beta + beta // 2 - 2 * (beta // 3)) % 4
-            term = jnp.dot(h[:, beta].reshape(512, UP_W), out_columns(w2, s), preferred_element_type=F32)
-            term = term.reshape(2, 2, 128, 256)
-            if k == 0:
-                acc[s, b] = term
-            else:
-                acc[s, b] += term
-            return carry
-
-        lax.fori_loop(0, 4 * N_OUT, tile, 0)
-
-    def finish_full():
-        columns_ready(mine_w2, partner_w2, 3)
-
-        def tile(i, carry):
-            d, s = i // N_OUT, i % N_OUT
-            term = jnp.dot(HF[d], out_columns(W2F, s), preferred_element_type=F32)
-            acc[s, d] += term.reshape(2, 2, 128, 256)
+            lhs = jnp.concatenate([HU[k, :, beta].reshape(512, UP_W) for k in range(2)], axis=1)
+            term = jnp.dot(lhs, out_columns(0, s), preferred_element_type=F32)
+            acc[s, block_at(beta)] = term.reshape(2, 2, 128, 256)
             return carry
 
         lax.fori_loop(0, 4 * N_OUT, tile, 0)
@@ -355,16 +352,16 @@
     core_msgs[0].wait_recv()
     produce(near[0])
     combine(near[0])
+    activate(near[0])
+    produce(near[1])
     gather_forward()
-    produce(near[1])
-    activate(near[0])
     combine(near[1])
     gather_near()
     produce(middle[0])
     produce(middle[1])
     forward(near[0])
+    combine(middle[0])
     activate(near[1])
-    combine(middle[0])
     combine(middle[1])
     gather_far()
     produce(far[0])
@@ -380,36 +377,35 @@
     forward(middle[0])
     forward(middle[1])
     combine(whole)
-    produce(full)
     forward(far[0])
     forward(far[1])
+    produce(full)
     activate(whole)
     combine(full)
     produce(shared)
     forward(whole)
+    landed(near[0], middle[0], far[0])
+    landed(near[1], middle[1], far[1])
+    combine(shared)
     activate(full)
-    combine(shared)
-    landed(near[0], middle[0], far[0])
-    finish_up(0)
+    second_product()
+    activate(shared)
     forward(full)
-    activate(shared)
-    landed(near[1], middle[1], far[1])
-    finish_up(1)
+    landed(whole)
     forward(shared)
-    landed(whole)
-    finish_up(2)
+    columns_ready(mine_w2, partner_w2, 1)
     landed(full)
-    finish_full()
     landed(shared)
-    columns_ready(mine_w2, partner_w2, 4)
 
     def out_core(s):
-        columns = out_columns(W2S, s)
-
-        def one(d, carry):
-            term = jnp.dot(HS[d], columns, preferred_element_type=F32)
-            acc[s, d, zh] += term.reshape(2, 128, 256)
-            OS[s, d] = acc[s, d, :, 1 - c].astype(BF16)
+        columns = out_columns(512, s)
+
+        def one(beta, carry):
+            b = block_at(beta)
+            lhs = jnp.concatenate([HU[2, :, beta].reshape(512, UP_W), HF[b], HS[b].reshape(512, HD)], axis=1)
+            term = jnp.dot(lhs, columns, preferred_element_type=F32).reshape(2, 2, 128, 256)
+            acc[s, b] += term
+            OS[s, b] = acc[s, b, :, 1 - c].astype(BF16)
             return carry
 
         lax.fori_loop(0, 4, one, 0)
@@ -471,19 +467,19 @@
 
     sequence = (0, 3, 1, 4, 2, 5)
     core, one, two = {}, {}, {}
-    for t in range(N_OUT + 8):
+    for t in range(N_OUT + 5):
         if t < N_OUT:
             core[t] = out_core(sequence[t])
         if 0 <= t - 1 < N_OUT:
             one[t - 1] = out_first(sequence[t - 1], core[t - 1])
+        if 0 <= t - 2 < N_OUT:
+            one[t - 2].third()
         if 0 <= t - 3 < N_OUT:
-            one[t - 3].third()
+            two[t - 3] = out_second(sequence[t - 3], one[t - 3])
+        if 0 <= t - 4 < N_OUT:
+            two[t - 4].third()
         if 0 <= t - 5 < N_OUT:
-            two[t - 5] = out_second(sequence[t - 5], one[t - 5])
-        if 0 <= t - 6 < N_OUT:
-            two[t - 6].third()
-        if 0 <= t - 8 < N_OUT:
-            out_last(sequence[t - 8], two[t - 8])
+            out_last(sequence[t - 5], two[t - 5])
     for copy in sent:
         copy.wait_send()
 
@@ -495,11 +491,11 @@
 def body(tokens, ln_gain, w_qkv, w_up, w_out, w_down):
     scratch = [
         vm(4, 2, 2, 128, 1536), vm(1536, 384), vm(1536, 384), vm(N_UP, 1536, UP_W),
-        vm(128, 1536), vm(128, 1536), vm(N_UP, UP_W, 1536),
+        vm(1024, 1536),
         vm(4, 512, 384), vm(4, 256, 384), vm(N_UP, 4, 4, 128, UP_W),
         vm(2, 256, 384), vm(2, 128, 384), vm(N_UP, 2, 2, 128, UP_W),
         vm(2, 512, 384), vm(2, 256, 384), vm(N_UP, 2, 4, 128, UP_W),
-        vm(4, 512, 128), vm(4, 256, 128), vm(N_UP, 4, 4, 128, UP_W),
+        vm(4, 512, 128), vm(4, 2, 256, 128), vm(N_UP, 4, 4, 128, UP_W),
         vm(N_OUT, 4, 2, 2, 128, 256, dtype=F32), vm(N_OUT, 4, 2, 128, 256), vm(N_OUT, 4, 2, 128, 256),
         vm(3, 2, 128, 256), vm(3, 2, 2, 128, 256), vm(3, 2, 128, 256), vm(3, 2, 64, 128), vm(3, 2, 2, 64, 128),
         vm(3, 2, 2, 128, 128), vm(3, 2, 2, 2, 128, 128), vm(3, 4, 128, 128), vm(3, 2, 64, 128), vm(3, 2, 2, 64, 128),

time: 174 us -> 162 us (0.931)
  Pallas kernels: 171 us -> 159 us
    pallas_call x1, Pallas kernels: 171 us -> 159 us  [body(): pl.pallas_call(kernel, out_shape=jax.ShapeDtypeStruct((128, KB), BF16), i...]
where the time goes in v3:
time: 162 us; the launch traced here: 161 us
  Pallas kernels  159 us (98%)
  local copies, waits for them, and re-layouts  1.62 us (1%)
    pallas_call x1, Pallas kernels, body(): pl.pallas_call(kernel, out_shape=jax.ShapeDtypeStruct((128, KB), BF16), i...  159 us

profile of v3, /device:TPU:0, one launch (start us, length us, event | category | flops | bytes accessed | tf_op | source)
XLA Modules:
  0.0 160.5 jit_solution(510261773391550549)
XLA Ops:
  0.0 158.9 %layer.1 = bf16[128,768]{1,0:T(8,128)(2,1)} custom-call(bf16[128,768]{1,0:T(8,128)(2,1)} %tok.1, f32[768]{0:T(1024)} %gain.1, bf16[3,768,384]{2,1,0:T(8,128)(2,1)} %bitcast.1, bf16[768,1536]{1,0:T(8,128)(2,1)} %wu.1, bf16[384,768]{1,0:T(8,128)(2,1)} %wo.1, bf16[1536,768]{1,0:T(8,128)(2,1)} %wd.1), custom_call_target="tpu_custom_call" | custom-call | tf_op jit(solution)/shard_map/layer/pallas_call | solution.py:506
  158.9 1.6 %copy.8 = bf16[128,768]{1,0:T(8,128)(2,1)} copy(bf16[128,768]{1,0:T(8,128)(2,1)} %layer.1) | data formatting | bytes 393216

commit v4 on v3

--- a/solution.py
+++ b/solution.py
@@ -73,13 +73,15 @@
 
 
 N_OUT = 6
+GROUPS = ((0, 1), (1, 2), (3, 1))
+BLOCK_OF = (0, 1, 3, 2)
 
 
 def kernel(
     tok, gain, wq, wu, wo, wd, out,
     X, W1F, W1S, W1U, W2,
     PF, PS, PU, AF, AS, AU, BF, BS, BU, HF, HS, HU,
-    acc, OS, OC, Y0A, Y0B, Z0P, Z0A, Z0B, Z1A, Z1B, Y1P, Y1A, Y1B,
+    acc, OS, OC, Y0A, Y0B, Z0P, Z0A, Z0B, Z1A, Z1B, Z2A, Z2B, Y1P, Y1A, Y1B,
     stats, send_sem, recv_sem, loc_sem,
 ):
     row, col = lax.axis_index("row"), lax.axis_index("col")
@@ -149,7 +151,7 @@
 
     def w1_parts(who):
         parts = [[(wu.at[:, up_part(who, k)], W1U.at[k, own_k])] for k in range(N_UP)]
-        return parts + [w1_full(who), w1_shared]
+        return parts[:2] + [w1_full(who), w1_shared, parts[2]]
 
     def w2_parts(who):
         return [
@@ -247,7 +249,8 @@
             send, x, xr, xl, lambda i, half: p.at[(i, *at(half))], a_l, a_r,
             [b.at[(0, *at(half))] for half in range(2)], [b.at[(1, *at(half))] for half in range(2)],
         )
-        return dict(kind=kind, k=k, p=p, h=h, at=at, base=base, blocks=blocks, ring=ring)
+        weights = 4 if kind == "up" and k == 2 else k
+        return dict(kind=kind, k=k, w=weights, p=p, h=h, at=at, base=base, blocks=blocks, ring=ring)
 
     def columns_ready(parts, partner, k):
         for copy in parts[k]:
@@ -257,7 +260,7 @@
         parts[k], partner[k] = [], []
 
     def produce(u):
-        columns_ready(mine_w1, partner_w1, u["k"])
+        columns_ready(mine_w1, partner_w1, u["w"])
         kind, ring, p = u["kind"], u["ring"], u["p"]
         if kind == "up":
             w1, blocks = W1U.at[u["k"]], u["blocks"]
@@ -338,7 +341,7 @@
             beta, s = i // N_OUT, i % N_OUT
             lhs = jnp.concatenate([HU[k, :, beta].reshape(512, UP_W) for k in range(2)], axis=1)
             term = jnp.dot(lhs, out_columns(0, s), preferred_element_type=F32)
-            acc[s, block_at(beta)] = term.reshape(2, 2, 128, 256)
+            acc[s, beta] = term.reshape(2, 2, 128, 256)
             return carry
 
         lax.fori_loop(0, 4 * N_OUT, tile, 0)
@@ -346,8 +349,8 @@
     near = [unit("up", k, 0) for k in range(2)]
     middle = [unit("up", k, 1) for k in range(2)]
     far = [unit("up", k, 2) for k in range(2)]
-    whole = unit("up", 2)
-    full, shared = unit("full", 3), unit("shared", 4)
+    last = [unit("up", 2, group) for group in range(3)]
+    full, shared = unit("full", 2), unit("shared", 3)
 
     core_msgs[0].wait_recv()
     produce(near[0])
@@ -371,115 +374,152 @@
     combine(far[0])
     activate(middle[1])
     combine(far[1])
-    produce(whole)
+    produce(full)
     activate(far[0])
     activate(far[1])
     forward(middle[0])
     forward(middle[1])
-    combine(whole)
+    combine(full)
     forward(far[0])
     forward(far[1])
-    produce(full)
-    activate(whole)
-    combine(full)
     produce(shared)
-    forward(whole)
+    activate(full)
+    combine(shared)
+    produce(last[2])
+    produce(last[1])
+    forward(full)
+    activate(shared)
+    combine(last[2])
+    combine(last[1])
+    produce(last[0])
     landed(near[0], middle[0], far[0])
     landed(near[1], middle[1], far[1])
-    combine(shared)
-    activate(full)
     second_product()
-    activate(shared)
-    forward(full)
-    landed(whole)
+    activate(last[2])
+    combine(last[0])
     forward(shared)
-    columns_ready(mine_w2, partner_w2, 1)
-    landed(full)
-    landed(shared)
-
-    def out_core(s):
-        columns = out_columns(512, s)
-
-        def one(beta, carry):
-            b = block_at(beta)
+    activate(last[1])
+    forward(last[2])
+    activate(last[0])
+    forward(last[1])
+
+    def out_core(group, path):
+        beta0, n = GROUPS[group]
+
+        def one(i, carry):
+            beta, j = beta0 + i // 3, i % 3
+            s, b = path * 3 + j, block_at(beta)
             lhs = jnp.concatenate([HU[2, :, beta].reshape(512, UP_W), HF[b], HS[b].reshape(512, HD)], axis=1)
-            term = jnp.dot(lhs, columns, preferred_element_type=F32).reshape(2, 2, 128, 256)
-            acc[s, b] += term
-            OS[s, b] = acc[s, b, :, 1 - c].astype(BF16)
+            term = jnp.dot(lhs, out_columns(512, s), preferred_element_type=F32)
+            acc[s, beta] += term.reshape(2, 2, 128, 256)
+            OS[path, beta, j] = acc[s, beta, :, 1 - c].astype(BF16)
             return carry
 
-        lax.fori_loop(0, 4, one, 0)
-        return send(OS.at[s], OC.at[s], sib)
-
-    def out_first(s, message):
+        lax.fori_loop(0, 3 * n, one, 0)
+        some = pl.ds(beta0, n)
+        return send(OS.at[path, some], OC.at[path, some], sib)
+
+    def out_add(group, path, message):
+        beta0, n = GROUPS[group]
         message.wait_recv()
 
-        def one(d, carry):
-            OC[s, d] = (OC[s, d].astype(F32) + acc[s, d, :, c]).astype(BF16)
+        def one(i, carry):
+            beta, j = beta0 + i // 3, i % 3
+            OC[path, beta, j] = (OC[path, beta, j].astype(F32) + acc[path * 3 + j, beta, :, c]).astype(BF16)
             return carry
 
-        lax.fori_loop(0, 4, one, 0)
-        if s < 3:
-            ring = Ring(
-                send, y, yr, yl, lambda i, half: OC.at[s, i, half], Y0A.at[s, 0], Y0A.at[s, 1],
-                [Y0B.at[s, 0, half] for half in range(2)], [Y0B.at[s, 1, half] for half in range(2)],
-            )
+        lax.fori_loop(0, 3 * n, one, 0)
+
+    def z_ring(group):
+        beta0, n = GROUPS[group]
+        if n == 1:
+            a, b = Z1A.at[beta0 // 3], Z1B.at[beta0 // 3]
+
+            def piece(i, half):
+                return OC.at[1, beta0, :, i % 2, pl.ds(64 * half, 64), part(128, i // 2)]
         else:
-            ring = Ring(
-                send, z, zr, zlft,
-                lambda i, half: OC.at[s, pl.ds(2 * half, 2), i % 2, :, part(128, i // 2)],
-                Z1A.at[s - 3, 0], Z1A.at[s - 3, 1],
-                [Z1B.at[s - 3, 0, half] for half in range(2)], [Z1B.at[s - 3, 1, half] for half in range(2)],
-            )
+            a, b = Z2A, Z2B
+
+            def piece(i, half):
+                return OC.at[1, beta0 + half, :, i % 2, :, part(128, i // 2)]
+
+        ring = Ring(
+            send, z, zr, zlft, piece, a.at[0], a.at[1],
+            [b.at[0, half] for half in range(2)], [b.at[1, half] for half in range(2)],
+        )
         ring.first()
         ring.second()
         return ring
 
-    def out_second(s, before):
-        before.arrive()
-        if s < 3:
-            for half in range(2):
-                Z0P[s, half] = before.total(half).astype(BF16)
-            ring = Ring(
-                send, z, zr, zlft,
-                lambda i, half: Z0P.at[s, i % 2, pl.ds(64 * half, 64), part(128, i // 2)],
-                Z0A.at[s, 0], Z0A.at[s, 1],
-                [Z0B.at[s, 0, half] for half in range(2)], [Z0B.at[s, 1, half] for half in range(2)],
-            )
-        else:
-            j = s - 3
-            for half in range(2):
-                Y1P[j, 2 * half : 2 * half + 2] = before.total(half).astype(BF16)
-            ring = Ring(
-                send, y, yr, yl, lambda i, half: Y1P.at[j, i, pl.ds(64 * half, 64)],
-                Y1A.at[j, 0], Y1A.at[j, 1],
-                [Y1B.at[j, 0, half] for half in range(2)], [Y1B.at[j, 1, half] for half in range(2)],
-            )
-        ring.first()
-        ring.second()
-        return ring
-
-    def out_last(s, ring):
+    def z_done(group, ring):
+        beta0, n = GROUPS[group]
         ring.arrive()
         for half in range(2):
-            rows, columns = slice(64 * half, 64 * half + 64), slice(128 * s, 128 * s + 128)
-            out[rows, columns] = (tok[rows, columns].astype(F32) + ring.total(half)).astype(BF16)
-
-    sequence = (0, 3, 1, 4, 2, 5)
-    core, one, two = {}, {}, {}
-    for t in range(N_OUT + 5):
-        if t < N_OUT:
-            core[t] = out_core(sequence[t])
-        if 0 <= t - 1 < N_OUT:
-            one[t - 1] = out_first(sequence[t - 1], core[t - 1])
-        if 0 <= t - 2 < N_OUT:
-            one[t - 2].third()
-        if 0 <= t - 3 < N_OUT:
-            two[t - 3] = out_second(sequence[t - 3], one[t - 3])
-        if 0 <= t - 4 < N_OUT:
-            two[t - 4].third()
-        if 0 <= t - 5 < N_OUT:
-            out_last(sequence[t - 5], two[t - 5])
+            if n == 1:
+                Y1P[beta0, :, 64 * half : 64 * half + 64] = ring.total(half).astype(BF16)
+            else:
+                Y1P[beta0 + half] = ring.total(half).astype(BF16)
+
+    y_first = Ring(
+        send, 0, yr, yl, lambda i, half: OC.at[0, BLOCK_OF[i], :, half], Y0A.at[0], Y0A.at[1],
+        [Y0B.at[0, half] for half in range(2)], [Y0B.at[1, half] for half in range(2)],
+    )
+    z_last = Ring(
+        send, z, zr, zlft, lambda i, half: Z0P.at[i % 2, :, pl.ds(64 * half, 64), part(128, i // 2)],
+        Z0A.at[0], Z0A.at[1],
+        [Z0B.at[0, half] for half in range(2)], [Z0B.at[1, half] for half in range(2)],
+    )
+    y_last = Ring(
+        send, 0, yr, yl, lambda i, half: Y1P.at[BLOCK_OF[i], :, pl.ds(64 * half, 64)], Y1A.at[0], Y1A.at[1],
+        [Y1B.at[0, half] for half in range(2)], [Y1B.at[1, half] for half in range(2)],
+    )
+
+    def out_last(path, ring):
+        ring.arrive()
+        for half in range(2):
+            total = ring.total(half)
+            for j in range(3):
+                rows, columns = slice(64 * half, 64 * half + 64), slice(128 * (3 * path + j), 128 * (3 * path + j + 1))
+                out[rows, columns] = (tok[rows, columns].astype(F32) + total[j]).astype(BF16)
+
+    columns_ready(mine_w2, partner_w2, 1)
+    landed(full, shared)
+    landed(last[2])
+    far_core = [out_core(2, path) for path in range(2)]
+    forward(last[0])
+    out_add(2, 0, far_core[0])
+    y_first.first()
+    out_add(2, 1, far_core[1])
+    far_z = z_ring(2)
+    landed(last[1])
+    mid_core = [out_core(1, path) for path in range(2)]
+    far_z.third()
+    out_add(1, 0, mid_core[0])
+    y_first.second()
+    out_add(1, 1, mid_core[1])
+    mid_z = z_ring(1)
+    y_first.third()
+    z_done(2, far_z)
+    y_last.first()
+    landed(last[0])
+    near_core = [out_core(0, path) for path in (1, 0)]
+    mid_z.third()
+    out_add(0, 1, near_core[0])
+    near_z = z_ring(0)
+    out_add(0, 0, near_core[1])
+    z_done(1, mid_z)
+    y_last.second()
+    near_z.third()
+    y_last.third()
+    y_first.arrive()
+    for half in range(2):
+        Z0P[half] = y_first.total(half).astype(BF16)
+    z_last.first()
+    z_last.second()
+    z_done(0, near_z)
+    z_last.third()
+    out_last(1, y_last)
+    out_last(0, z_last)
     for copy in sent:
         copy.wait_send()
 
@@ -496,9 +536,10 @@
         vm(2, 256, 384), vm(2, 128, 384), vm(N_UP, 2, 2, 128, UP_W),
         vm(2, 512, 384), vm(2, 256, 384), vm(N_UP, 2, 4, 128, UP_W),
         vm(4, 512, 128), vm(4, 2, 256, 128), vm(N_UP, 4, 4, 128, UP_W),
-        vm(N_OUT, 4, 2, 2, 128, 256, dtype=F32), vm(N_OUT, 4, 2, 128, 256), vm(N_OUT, 4, 2, 128, 256),
-        vm(3, 2, 128, 256), vm(3, 2, 2, 128, 256), vm(3, 2, 128, 256), vm(3, 2, 64, 128), vm(3, 2, 2, 64, 128),
-        vm(3, 2, 2, 128, 128), vm(3, 2, 2, 2, 128, 128), vm(3, 4, 128, 128), vm(3, 2, 64, 128), vm(3, 2, 2, 64, 128),
+        vm(N_OUT, 4, 2, 2, 128, 256, dtype=F32), vm(2, 4, 3, 2, 128, 256), vm(2, 4, 3, 2, 128, 256),
+        vm(2, 3, 128, 256), vm(2, 2, 3, 128, 256), vm(2, 3, 128, 256), vm(2, 3, 64, 128), vm(2, 2, 3, 64, 128),
+        vm(2, 2, 3, 64, 128), vm(2, 2, 2, 3, 64, 128), vm(2, 3, 128, 128), vm(2, 2, 3, 128, 128),
+        vm(4, 3, 128, 128), vm(2, 3, 64, 128), vm(2, 2, 3, 64, 128),
         vm(8, 16, 128, dtype=F32),
         pltpu.SemaphoreType.DMA((N_MSG,)), pltpu.SemaphoreType.DMA((N_MSG,)), pltpu.SemaphoreType.DMA((N_LOC,)),
     ]

time: 162 us -> 154 us (0.951)
  Pallas kernels: 159 us -> 152 us
    pallas_call x1, Pallas kernels: 159 us -> 152 us  [body(): pl.pallas_call(kernel, out_shape=jax.ShapeDtypeStruct((128, KB), BF16), i...]
where the time goes in v4:
time: 154 us
  Pallas kernels  152 us (99%)
  local copies, waits for them, and re-layouts  1.62 us (1%)
    pallas_call x1, Pallas kernels, body(): pl.pallas_call(kernel, out_shape=jax.ShapeDtypeStruct((128, KB), BF16), i...  152 us

profile of v4, /device:TPU:0, one launch (start us, length us, event | category | flops | bytes accessed | tf_op | source)
XLA Modules:
  0.0 153.8 jit_solution(15279856936303010993)
XLA Ops:
  0.0 152.2 %layer.1 = bf16[128,768]{1,0:T(8,128)(2,1)} custom-call(bf16[128,768]{1,0:T(8,128)(2,1)} %tok.1, f32[768]{0:T(1024)} %gain.1, bf16[3,768,384]{2,1,0:T(8,128)(2,1)} %bitcast.1, bf16[768,1536]{1,0:T(8,128)(2,1)} %wu.1, bf16[384,768]{1,0:T(8,128)(2,1)} %wo.1, bf16[1536,768]{1,0:T(8,128)(2,1)} %wd.1), custom_call_target="tpu_custom_call" | custom-call | tf_op jit(solution)/shard_map/layer/pallas_call | solution.py:547
  152.2 1.6 %copy.8 = bf16[128,768]{1,0:T(8,128)(2,1)} copy(bf16[128,768]{1,0:T(8,128)(2,1)} %layer.1) | data formatting | bytes 393216

commit v5 on v4

--- a/solution.py
+++ b/solution.py
@@ -16,7 +16,7 @@
 N_UP = 3
 UP_W = 256
 N_MSG = 256
-N_LOC = 24
+N_LOC = 40
 
 
 def head_norm(v):
@@ -79,7 +79,7 @@
 
 def kernel(
     tok, gain, wq, wu, wo, wd, out,
-    X, W1F, W1S, W1U, W2,
+    X, W1F, W1S, W1U, W2, TU, TF, TS, T2,
     PF, PS, PU, AF, AS, AU, BF, BS, BU, HF, HS, HU,
     acc, OS, OC, Y0A, Y0B, Z0P, Z0A, Z0B, Z1A, Z1B, Z2A, Z2B, Y1P, Y1A, Y1B,
     stats, send_sem, recv_sem, loc_sem,
@@ -134,6 +134,33 @@
 
     own_k = part(KB, zh)
 
+    def up_part(who, k):
+        return pl.ds(pl.multiple_of(who * KB + k * UP_W, UP_W), UP_W)
+
+    def w1_parts(who, u, f, s):
+        parts = [[(wu.at[:, up_part(who, k)], u(k))] for k in range(N_UP)]
+        heads = [(wq.at[j, :, part(HD, 2 * who)], f(pl.ds(j * HD, HD))) for j in range(3)]
+        shared = [(wq.at[j, :, pl.ds(HD, HD)], s(pl.ds(j * HD, HD))) for j in range(3)]
+        return parts[:2] + [heads, shared, parts[2]]
+
+    def w2_parts(who, at):
+        return [
+            [(wd.at[pl.ds(pl.multiple_of(who * KB, KB), 512)], at(pl.ds(0, 512)))],
+            [
+                (wd.at[up_part(who, 2)], at(pl.ds(512, UP_W))),
+                (wo.at[part(HD, 2 * who)], at(pl.ds(768, HD))),
+                (wo.at[pl.ds(HD, HD)], at(pl.ds(896, HD))),
+            ],
+        ]
+
+    staged = w1_parts(zo, lambda k: TU.at[k], lambda cols: TF.at[:, cols], lambda cols: TS.at[:, cols])
+    staged = [[local(*p) for p in ps] for ps in staged + w2_parts(zo, lambda rows: T2.at[rows])]
+    mine_w1 = w1_parts(
+        zh, lambda k: W1U.at[k, own_k], lambda cols: W1F.at[own_k, cols], lambda cols: W1S.at[own_k, cols]
+    )
+    mine_w1 = [[local(*p) for p in ps] for ps in mine_w1]
+    mine_w2 = [[local(*p) for p in ps] for ps in w2_parts(zh, lambda rows: W2.at[zh, rows])]
+
     values = tok[...].astype(F32)
     sums = [jnp.sum(values, axis=-1, keepdims=True), jnp.sum(values * values, axis=-1, keepdims=True)]
     for i, s in enumerate(sums):
@@ -141,31 +168,23 @@
     pl.semaphore_wait(barrier, len(everyone))
     moments = [send(stats.at[0], stats.at[i + 1], who) for i, who in enumerate(row_others)]
 
-    def w1_full(who):
-        return [(wq.at[j, :, part(HD, 2 * who)], W1F.at[own_k, pl.ds(j * HD, HD)]) for j in range(3)]
-
-    w1_shared = [(wq.at[j, :, pl.ds(HD, HD)], W1S.at[own_k, pl.ds(j * HD, HD)]) for j in range(3)]
-
-    def up_part(who, k):
-        return pl.ds(pl.multiple_of(who * KB + k * UP_W, UP_W), UP_W)
-
-    def w1_parts(who):
-        parts = [[(wu.at[:, up_part(who, k)], W1U.at[k, own_k])] for k in range(N_UP)]
-        return parts[:2] + [w1_full(who), w1_shared, parts[2]]
-
-    def w2_parts(who):
-        return [
-            [(wd.at[pl.ds(pl.multiple_of(who * KB, KB), 512)], W2.at[pl.ds(0, 512), own_k])],
-            [
-                (wd.at[up_part(who, 2)], W2.at[pl.ds(512, UP_W), own_k]),
-                (wo.at[part(HD, 2 * who)], W2.at[pl.ds(768, HD), own_k]),
-                (wo.at[pl.ds(HD, HD)], W2.at[pl.ds(896, HD), own_k]),
-            ],
-        ]
-
-    partner_w1 = [[send(*p, zp) for p in ps] for ps in w1_parts(zo)[:1]]
-    mine_w1 = [[local(*p) for p in ps] for ps in w1_parts(zh)]
-    mine_w2 = [[local(*p) for p in ps] for ps in w2_parts(zh)]
+    partner_w1, partner_w2 = [], []
+    to_partner = [
+        (partner_w1, TU.at[0], W1U.at[0, own_k]), (partner_w1, TU.at[1], W1U.at[1, own_k]),
+        (partner_w1, TF, W1F.at[own_k]), (partner_w1, TS, W1S.at[own_k]),
+        (partner_w1, TU.at[2], W1U.at[2, own_k]),
+        (partner_w2, T2.at[pl.ds(0, 512)], W2.at[zh, pl.ds(0, 512)]),
+        (partner_w2, T2.at[pl.ds(512, 512)], W2.at[zh, pl.ds(512, 512)]),
+    ]
+
+    def next_weights(n=1):
+        for _ in range(n):
+            into, src, dst = to_partner.pop(0)
+            for copy in staged[7 - len(to_partner) - 1]:
+                copy.wait()
+            into.append([send(src, dst, zp)])
+
+    next_weights(1)
     for m in moments:
         m.wait_recv()
     all_sums = jnp.sum(stats[...], axis=0) / D
@@ -177,8 +196,7 @@
 
     own = X.at[y, zl, c, :, own_k]
     z_msgs = {3: send(own, own, zr), 1: send(own, own, zlft), 2: send(own, own, zp)}
-    partner_w1 += [[send(*p, zp) for p in ps] for ps in w1_parts(zo)[1:]]
-    partner_w2 = [[send(*p, zp) for p in ps] for ps in w2_parts(zo)]
+    next_weights(1)
 
     def x_piece(y_, step):
         z_ = (z + step) % 4
@@ -327,9 +345,8 @@
             u["f_l"].wait_recv()
 
     def out_columns(first, s):
-        rows = pl.ds(first, 512)
-        left, right = part(128, s), pl.ds(pl.multiple_of(KB + s * 128, 128), 128)
-        return jnp.concatenate([W2[rows, left], W2[rows, right]], axis=1)
+        rows, columns = pl.ds(first, 512), part(128, s)
+        return jnp.concatenate([W2[0, rows, columns], W2[1, rows, columns]], axis=1)
 
     def block_at(beta):
         return (y + beta + beta // 2 - 2 * (beta // 3)) % 4
@@ -354,12 +371,14 @@
 
     core_msgs[0].wait_recv()
     produce(near[0])
+    next_weights(1)
     combine(near[0])
+    gather_forward()
     activate(near[0])
     produce(near[1])
-    gather_forward()
     combine(near[1])
     gather_near()
+    next_weights(1)
     produce(middle[0])
     produce(middle[1])
     forward(near[0])
@@ -367,6 +386,7 @@
     activate(near[1])
     combine(middle[1])
     gather_far()
+    next_weights(1)
     produce(far[0])
     produce(far[1])
     forward(near[1])
@@ -375,6 +395,7 @@
     activate(middle[1])
     combine(far[1])
     produce(full)
+    next_weights(1)
     activate(far[0])
     activate(far[1])
     forward(middle[0])
@@ -383,6 +404,7 @@
     forward(far[0])
     forward(far[1])
     produce(shared)
+    next_weights(1)
     activate(full)
     combine(shared)
     produce(last[2])
@@ -531,7 +553,8 @@
 def body(tokens, ln_gain, w_qkv, w_up, w_out, w_down):
     scratch = [
         vm(4, 2, 2, 128, 1536), vm(1536, 384), vm(1536, 384), vm(N_UP, 1536, UP_W),
-        vm(1024, 1536),
+        vm(2, 1024, KB),
+        vm(N_UP, KB, UP_W), vm(KB, 384), vm(KB, 384), vm(1024, KB),
         vm(4, 512, 384), vm(4, 256, 384), vm(N_UP, 4, 4, 128, UP_W),
         vm(2, 256, 384), vm(2, 128, 384), vm(N_UP, 2, 2, 128, UP_W),
         vm(2, 512, 384), vm(2, 256, 384), vm(N_UP, 2, 4, 128, UP_W),

time: 154 us -> 154 us (level)
  no operation moved by 1% of the time
where the time goes in v5:
time: 154 us
  Pallas kernels  152 us (99%)
  local copies, waits for them, and re-layouts  1.62 us (1%)
    pallas_call x1, Pallas kernels, body(): pl.pallas_call(kernel, out_shape=jax.ShapeDtypeStruct((128, KB), BF16), i...  152 us

profile of v5, /device:TPU:0, one launch (start us, length us, event | category | flops | bytes accessed | tf_op | source)
XLA Modules:
  0.0 153.8 jit_solution(8593338726406908744)
XLA Ops:
  0.0 152.1 %layer.1 = bf16[128,768]{1,0:T(8,128)(2,1)} custom-call(bf16[128,768]{1,0:T(8,128)(2,1)} %tok.1, f32[768]{0:T(1024)} %gain.1, bf16[3,768,384]{2,1,0:T(8,128)(2,1)} %bitcast.1, bf16[768,1536]{1,0:T(8,128)(2,1)} %wu.1, bf16[384,768]{1,0:T(8,128)(2,1)} %wo.1, bf16[1536,768]{1,0:T(8,128)(2,1)} %wd.1), custom_call_target="tpu_custom_call" | custom-call | tf_op jit(solution)/shard_map/layer/pallas_call | solution.py:570
  152.2 1.6 %copy.8 = bf16[128,768]{1,0:T(8,128)(2,1)} copy(bf16[128,768]{1,0:T(8,128)(2,1)} %layer.1) | data formatting | bytes 393216
